TPU v7x, 256 devices: a whole 4x4x8 slice. The times are simulated.
256 devices in a mesh: seq: 32 (over y, z_lo, core), tp: 4 (over x), dp: 2 (over z_hi).
Axes of the slice: x: 4, y: 4, z: 8 (z_hi: 2, z_lo: 4; z = z_hi * 4 + z_lo), core: 2. Of those that a mesh axis runs over, the one named last changes fastest.
Arguments:
- frames: bfloat16 [16384, 2048], P(('dp', 'seq')), parts along dimension 0, may hold values from -6 to 6
- w_query: bfloat16 [2048, 2048], P(None, 'tp'), may hold values from -0.70710678 to 0.70710678
- w_key: bfloat16 [2048, 1024], P(None, 'tp'), may hold values from -0.70710678 to 0.70710678
- w_value: bfloat16 [2048, 1024], P(None, 'tp'), may hold values from -0.125 to 0.125
- w_out: bfloat16 [2048, 2048], P('tp'), may hold values from -0.125 to 0.125
- frame_pick: int32 [64, 32, 1], P(('dp', 'seq')), parts along dimension 0, may hold values from 0 to 255
- codes: int32 [2048, 32], P(('dp', 'seq')), parts along dimension 0, may hold values from 0 to 1023
- geo_ids: int32 [2048], P(('dp', 'seq')), parts along dimension 0, may hold values from 0 to 63
- geo_table: bfloat16 [64, 1024], replicated, may hold values from -6 to 6
- w_context: bfloat16 [2048, 1024], P('tp'), may hold values from -0.125 to 0.125
- code_table: bfloat16 [1024, 1024], replicated, may hold values from -6 to 6
- level_table: bfloat16 [32, 1024], replicated, may hold values from -6 to 6
- wd_query: bfloat16 [1024, 1024], P(None, 'tp'), may hold values from -1.25 to 1.25
- wd_key: bfloat16 [1024, 1024], P(None, 'tp'), may hold values from -1.25 to 1.25
- wd_value: bfloat16 [1024, 1024], P(None, 'tp'), may hold values from -0.1875 to 0.1875
- wd_out: bfloat16 [1024, 1024], P('tp'), may hold values from -0.1875 to 0.1875
Outputs:
- temporal: bfloat16 [16384, 2048], P(('dp', 'seq'), 'tp'), parts along dimension 0
- depth: bfloat16 [2048, 32, 1024], P(('dp', 'seq'), None, 'tp'), parts along dimension 0
There are 2 independent parts, one for each index of `dp`. A program takes and returns all parts, laid end to end along the dimension named above; an argument that names none is the same for every part. Nothing has to cross between parts.
All inputs are finite; a program needn't handle non-finite values.
Results may differ from a plain program's by a relative error of at most 0.022.
Values may be sent and summed in bfloat16 or wider, within the bound.
A program may use at most 128 MiB of HBM per device.

v0:
```python
import jax
import jax.numpy as jnp
from jax import lax
from jax.sharding import PartitionSpec as P

HEAD = 128
DHEAD = 64
GEO_VOCAB = 64


def rms_rows(values, epsilon):
    return values * lax.rsqrt(jnp.mean(values * values, axis=-1, keepdims=True) + epsilon)


def body(
    frames,
    w_query,
    w_key,
    w_value,
    w_out,
    frame_pick,
    codes,
    geo_ids,
    geo_table,
    w_context,
    code_table,
    level_table,
    wd_query,
    wd_key,
    wd_value,
    wd_out,
):
    tp_count = lax.axis_size("tp")
    seq_count = lax.axis_size("seq")
    seq_rank = lax.axis_index("seq")
    tp_rank = lax.axis_index("tp")
    frame_rows = frames.shape[0]
    width = frames.shape[1]
    width_local = width // tp_count
    kv_local = w_key.shape[1] // HEAD
    heads_local = w_query.shape[1] // HEAD
    group = heads_local // kv_local
    normed = rms_rows(frames.astype(jnp.float32), 1e-05).astype(jnp.bfloat16)
    queries = jnp.dot(normed, w_query, preferred_element_type=jnp.float32).astype(jnp.bfloat16)
    keys_local = jnp.dot(normed, w_key, preferred_element_type=jnp.float32).astype(jnp.bfloat16)
    values_local = jnp.dot(normed, w_value, preferred_element_type=jnp.float32).astype(jnp.bfloat16)
    queries_grouped = queries.reshape(frame_rows, kv_local, group, HEAD)
    first_query = seq_rank * frame_rows
    last_query = first_query + frame_rows - 1
    query_pos = first_query + jnp.arange(frame_rows, dtype=jnp.int32)

    def fold_piece(carry, piece, masked):
        top_old, total_old, accum_old = carry
        piece_rows = piece[0].shape[0]
        keys_piece = piece[0].reshape(piece_rows, kv_local, HEAD)
        values_piece = piece[1].reshape(piece_rows, kv_local, HEAD)
        scores = jnp.einsum(
            "qcgd,kcd->cgqk", queries_grouped, keys_piece, preferred_element_type=jnp.float32
        ) * HEAD ** (-0.5)
        if masked:
            key_pos = jnp.arange(piece_rows, dtype=jnp.int32)
            causal = key_pos[None, :] <= query_pos[:, None]
            scores = jnp.where(causal, scores, jnp.float32(-1e30))
        top_new = jnp.maximum(top_old, jnp.max(scores, axis=-1))
        factor = jnp.exp(top_old - top_new)
        weights = jnp.exp(scores - top_new[..., None])
        if masked:
            weights = jnp.where(causal, weights, jnp.float32(0.0))
        total_new = total_old * factor + jnp.sum(weights, axis=-1)
        contrib = jnp.einsum(
            "cgqk,kcd->cgqd",
            weights.astype(jnp.bfloat16),
            values_piece,
            preferred_element_type=jnp.float32,
        )
        accum_new = accum_old * factor[..., None] + contrib
        return (top_new, total_new, accum_new)

    def attend_piece(carry, piece, start):
        piece_rows = piece[0].shape[0]

        def skipped(state):
            return state

        def below(state):
            return fold_piece(state, piece, False)

        def diagonal(state):
            return fold_piece(state, piece, True)

        which = jnp.where(
            start > last_query, 0, jnp.where(start + piece_rows - 1 <= first_query, 1, 2)
        ).astype(jnp.int32)
        return lax.switch(which, [skipped, below, diagonal], carry)

    start_state = (
        jnp.full((kv_local, group, frame_rows), -1e30, jnp.float32),
        jnp.zeros((kv_local, group, frame_rows), jnp.float32),
        jnp.zeros((kv_local, group, frame_rows, HEAD), jnp.float32),
    )
    top_final, total_final, accum_final = attend_piece(
        start_state,
        (
            lax.all_gather(keys_local, "seq", axis=0, tiled=True),
            lax.all_gather(values_local, "seq", axis=0, tiled=True),
        ),
        jnp.int32(0),
    )
    heads_out = rms_rows(accum_final / total_final[..., None], 1e-06)
    attended = (
        jnp.transpose(heads_out, (2, 0, 1, 3))
        .reshape(frame_rows, heads_local * HEAD)
        .astype(jnp.bfloat16)
    )
    partial_out = jnp.dot(attended, w_out, preferred_element_type=jnp.float32)
    summed_all = lax.psum(partial_out.astype(jnp.bfloat16), "tp").astype(jnp.float32)
    summed_mine = lax.dynamic_slice_in_dim(summed_all, tp_rank * width_local, width_local, 1)
    frames_mine = lax.dynamic_slice_in_dim(frames, tp_rank * width_local, width_local, 1).astype(
        jnp.float32
    )
    temporal = (frames_mine + summed_mine).astype(jnp.bfloat16)
    pick_count = frame_pick.shape[2]
    pick_rows = frame_pick.reshape(seq_count * pick_count)
    slab_rows = codes.shape[0]
    levels = codes.shape[1]
    depth_width = code_table.shape[1]
    chosen = jnp.take(temporal, pick_rows, axis=0).reshape(seq_count, pick_count, width_local)
    arrived = lax.all_to_all(chosen, "seq", split_axis=0, concat_axis=0, tiled=True).reshape(
        slab_rows, width_local
    )
    context_part = jnp.dot(arrived, w_context, preferred_element_type=jnp.float32)
    context = lax.psum(context_part.astype(jnp.bfloat16), "tp")
    code_rows = jnp.take(code_table, codes[:, :-1], axis=0).astype(jnp.float32)
    code_rows = jnp.concatenate(
        [jnp.zeros((slab_rows, 1, depth_width), jnp.float32), code_rows], axis=1
    )
    geo_onehot = (geo_ids[:, None] == jnp.arange(GEO_VOCAB, dtype=jnp.int32)[None, :]).astype(
        jnp.bfloat16
    )
    geo_rows = jnp.dot(geo_onehot, geo_table, preferred_element_type=jnp.float32)
    hidden = (
        context.astype(jnp.float32)[:, None, :]
        + level_table.astype(jnp.float32)[None]
        + geo_rows[:, None, :]
        + code_rows
    )
    depth_normed = (
        rms_rows(hidden, 1e-05).astype(jnp.bfloat16).reshape(slab_rows * levels, depth_width)
    )
    dheads_local = wd_query.shape[1] // DHEAD
    shape_heads = (slab_rows, levels, dheads_local, DHEAD)
    depth_queries = (
        jnp.dot(depth_normed, wd_query, preferred_element_type=jnp.float32)
        .astype(jnp.bfloat16)
        .reshape(shape_heads)
    )
    depth_keys = (
        jnp.dot(depth_normed, wd_key, preferred_element_type=jnp.float32)
        .astype(jnp.bfloat16)
        .reshape(shape_heads)
    )
    depth_values = (
        jnp.dot(depth_normed, wd_value, preferred_element_type=jnp.float32)
        .astype(jnp.bfloat16)
        .reshape(shape_heads)
    )
    scores = jnp.einsum(
        "flhd,fmhd->fhlm", depth_queries, depth_keys, preferred_element_type=jnp.float32
    ) * DHEAD ** (-0.5)
    levels_pos = jnp.arange(levels, dtype=jnp.int32)
    causal = levels_pos[None, :] <= levels_pos[:, None]
    scores = jnp.where(causal, scores, jnp.float32(-1e30))
    top_score = jnp.max(scores, axis=-1, keepdims=True)
    weights = jnp.where(causal, jnp.exp(scores - top_score), jnp.float32(0.0))
    totals = jnp.sum(weights, axis=-1)
    heads_sum = jnp.einsum(
        "fhlm,fmhd->flhd",
        weights.astype(jnp.bfloat16),
        depth_values,
        preferred_element_type=jnp.float32,
    )
    heads_depth = rms_rows(heads_sum / jnp.transpose(totals, (0, 2, 1))[:, :, :, None], 1e-06)
    depth_attended = heads_depth.astype(jnp.bfloat16).reshape(
        slab_rows * levels, dheads_local * DHEAD
    )
    depth_part = jnp.dot(depth_attended, wd_out, preferred_element_type=jnp.float32)
    depth_local = depth_width // tp_count
    depth_all = lax.psum(depth_part.astype(jnp.bfloat16), "tp").astype(jnp.float32)
    depth_mine = lax.dynamic_slice_in_dim(depth_all, tp_rank * depth_local, depth_local, 1)
    hidden_mine = lax.dynamic_slice_in_dim(hidden, tp_rank * depth_local, depth_local, 2)
    depth = (hidden_mine + depth_mine.reshape(slab_rows, levels, depth_local)).astype(jnp.bfloat16)
    return (temporal, depth)


def solution(mesh):
    return jax.shard_map(
        body,
        mesh=mesh,
        in_specs=(
            P(("dp", "seq"), None),
            P(None, "tp"),
            P(None, "tp"),
            P(None, "tp"),
            P("tp", None),
            P(("dp", "seq"), None, None),
            P(("dp", "seq"), None),
            P(("dp", "seq")),
            P(),
            P("tp", None),
            P(),
            P(),
            P(None, "tp"),
            P(None, "tp"),
            P(None, "tp"),
            P("tp", None),
        ),
        out_specs=(P(("dp", "seq"), "tp"), P(("dp", "seq"), None, "tp")),
        check_vma=False,
    )
```

profile of v0, /device:TPU:1, one launch (start us, length us, event | category | flops | bytes accessed | tf_op | source)
XLA Modules:
  0.0 429.1 jit_solution(4905638689405498630)
XLA Ops:
  7.2 1.7 fusion.36
  8.9 2.7 convolution_convert_fusion.7
  11.7 2.7 convolution_convert_fusion.6
  14.5 2.3 convolution_convert_fusion.5
  17.0 5.3 %gather_fusion.1 = bf16[992,1024]{1,0:T(8,128)(2,1)} fusion(bf16[1024,1024]{1,0:T(8,128)(2,1)S(1)} %copy-done, s32[1024]{0:T(1024)S(1)} %pad_clamp_fusion), kind=kCustom, calls=%fused_computation.1 | custom fusion | bytes 4067200 | tf_op jit(solution)/shard_map/jit(_take)/gather | solution.py:133
  22.4 2.9 reshape.183
  25.3 53.7 %all-gather.3.cloned.1.call-done = bf16[8192,256]{1,0:T(8,128)(2,1)} async-done(((bf16[256,256]{1,0:T(8,128)(2,1)}), bf16[8192,256]{1,0:T(8,128)(2,1)}) %all-gather.3.cloned.1.call-update) | async-done | bytes 4194320 | tf_op jit(solution)/shard_map/all_gather | solution.py:104
  78.9 64.3 %all-gather.5.cloned.1.call-done = bf16[8192,256]{1,0:T(8,128)(2,1)} async-done(((bf16[256,256]{1,0:T(8,128)(2,1)}), bf16[8192,256]{1,0:T(8,128)(2,1)}) %all-gather.5.cloned.1.call-update) | async-done | bytes 4194320 | tf_op jit(solution)/shard_map/all_gather | solution.py:105
  143.2 65.0 %conditional.1 = (f32[2,2,256]{2,1,0:T(2,128)S(1)}, f32[2,2,256,128]{2,3,1,0:T(8,128)S(1)}) conditional(s32[]{:T(128)} %clamp.3, () %tuple.20, (bf16[8192,256]{1,0:T(8,128)(2,1)}, bf16[256,2,2,128]{3,2,1,0:T(2,128)(2,1)S(1)}, bf16[8192,256]{1,0:T(8,128)(2,1)}) %tuple.21, (s32[]{:T(128)}, s32[256]{0:T(256)S(1)}, ...), branch_computations={%region_1.2_spmd, %region_2.5_spmd, %region_5.8_spmd} | conditional | flops 4406250496 | bytes 136100880 | solution.py:94
  144.6 6.9 %reshape.152 = bf16[8192,2,128]{2,1,0:T(2,128)(2,1)} reshape(bf16[8192,256]{1,0:T(8,128)(2,1)} %get-tuple-element.23) | data formatting | bytes 8388608 | tf_op jit(solution)/shard_map/cond/branch_2_fun/reshape | solution.py:55
  151.5 15.8 %fusion.16 = (f32[2,2,256]{2,1,0:T(2,128)S(1)}, f32[2,8192,256,2]{2,1,3,0:T(8,128)}) fusion(pred[256,8192]{0,1:T(8,128)(4,1)S(1)} %iota_compare_fusion, bf16[256,2,2,128]{3,2,1,0:T(2,128)(2,1)S(1)} %get-tuple-element.62, bf16[8192,2,128,1]{2,1,0,3:T(2,128)(2,1)} %bitcast.67), kind=kOutput, calls=%fused_computation.19 | convolution fusion | flops 2172648448 | bytes 40112128 | tf_op jit(solution)/shard_map/cond/branch_2_fun/qcgd,kcd->cgqk/dot_general | solution.py:57
  167.3 15.0 %fusion.18 = f32[2,2,256]{2,1,0:T(2,128)S(1)} fusion(f32[2,8192,256,2]{2,1,3,0:T(8,128)} %get-tuple-element.72, f32[2,2,256]{2,1,0:T(2,128)S(1)} %broadcast_maximum_fusion.1, pred[256,8192]{0,1:T(8,128)(4,1)S(1)} %iota_compare_fusion), kind=kLoop, calls=%fused_computation.21 | loop fusion | flops 41942016 | bytes 35659776 | tf_op jit(solution)/shard_map/cond/branch_2_fun/reduce_sum | solution.py:69
  182.3 6.9 %reshape.153 = bf16[8192,2,128]{2,1,0:T(2,128)(2,1)} reshape(bf16[8192,256]{1,0:T(8,128)(2,1)} %get-tuple-element.25) | data formatting | bytes 8388608 | tf_op jit(solution)/shard_map/cond/branch_2_fun/reshape | solution.py:56
  189.2 18.8 %fusion.25 = f32[2,2,256,128]{3,2,1,0:T(8,128)S(1)} fusion(bf16[8192,2,128,1]{2,1,0,3:T(2,128)(2,1)} %bitcast.66, f32[2,8192,256,2]{2,1,3,0:T(8,128)} %get-tuple-element.72, f32[2,2,256]{2,1,0:T(2,128)S(1)} %broadcast_maximum_fusion.1, pred[256,8192]{0,1:T(8,128)(4,1)S(1)} %iota_compare_fusion, f32[2,2,256]{2,1,0:T(2,128)S(1)} %get-tuple-element.69), kind=kOutput, calls=%fused_computation.28 | convolution fusion | flops 2189557760 | bytes 40378368 | tf_op jit(solution)/shard_map/cond/branch_2_fun/cgqk,kcd->cgqd/dot_general | solution.py:70
  208.4 3.4 convolution_convert_fusion
  211.8 1.9 broadcast_select_fusion
  213.8 46.2 %all-reduce.5.cloned.1.call-done = bf16[256,2048]{1,0:T(8,128)(2,1)} async-done(((bf16[256,2048]{1,0:T(8,128)(2,1)}), bf16[256,2048]{1,0:T(8,128)(2,1)}) %all-reduce.5.cloned.1.call-update) | async-done | bytes 1048592 | tf_op jit(solution)/shard_map/psum | solution.py:116
  263.6 9.5 %all-to-all-start = ((bf16[32,2,256]{2,1,0:T(2,128)(2,1)}), bf16[32,2,256]{2,1,0:T(2,128)(2,1)S(1)}, u32[]{:S(2)}, u32[]{:S(2)}) async-start(bf16[32,2,256]{2,1,0:T(2,128)(2,1)} %reshape.196), calls=%async_computation | async-start | bytes 65536 | tf_op jit(solution)/shard_map/all_to_all | solution.py:128
  275.1 5.5 %all-to-all-done = bf16[32,2,256]{2,1,0:T(2,128)(2,1)S(1)} async-done(((bf16[32,2,256]{2,1,0:T(2,128)(2,1)}), bf16[32,2,256]{2,1,0:T(2,128)(2,1)S(1)}, u32[]{:S(2)}, u32[]{:S(2)}) %all-to-all-start) | async-done | bytes 32800 | tf_op jit(solution)/shard_map/all_to_all | solution.py:128
  281.6 40.3 %all-reduce.7.cloned.1.call-done = bf16[32,1024]{1,0:T(8,128)(2,1)} async-done(((bf16[32,1024]{1,0:T(8,128)(2,1)}), bf16[32,1024]{1,0:T(8,128)(2,1)}) %all-reduce.7.cloned.1.call-update) | async-done | bytes 65552 | tf_op jit(solution)/shard_map/psum | solution.py:132
  322.8 3.2 convert_add_fusion
  326.0 1.6 multiply_convert_fusion
  330.0 3.3 convolution_convert_fusion.3
  333.3 2.8 reshape.170
  336.1 2.5 convolution_convert_fusion.4
  338.6 2.0 reshape.169
  340.7 3.4 fusion.57
  344.1 2.7 multiply_reduce_fusion.1
  348.1 1.5 reshape.172
  349.6 3.3 convolution_convert_fusion.1
  352.9 66.4 %all-reduce.9.cloned.1.call-done = bf16[1024,1024]{1,0:T(8,128)(2,1)} async-done(((bf16[1024,1024]{1,0:T(8,128)(2,1)}), bf16[1024,1024]{1,0:T(8,128)(2,1)}) %all-reduce.9.cloned.1.call-update) | async-done | bytes 2097168 | tf_op jit(solution)/shard_map/psum | solution.py:188
  420.4 2.2 add_convert_fusion
  (69 shorter events, 14.5 us)
Async XLA Ops:
  7.2 9.9 %copy-start = (bf16[1024,1024]{1,0:T(8,128)(2,1)S(1)}, bf16[1024,1024]{1,0:T(8,128)(2,1)}, u32[]{:S(2)}) copy-start(bf16[1024,1024]{1,0:T(8,128)(2,1)} %param.29) | copy-start | bytes 6291460
  7.2 7.3 %copy-start.4 = (bf16[256,2048]{1,0:T(8,128)(2,1)S(1)}, bf16[256,2048]{1,0:T(8,128)(2,1)}, u32[]{:S(2)}) copy-start(bf16[256,2048]{1,0:T(8,128)(2,1)} %param.19) | copy-start | bytes 3145732
  7.2 71.7 %all-gather.3.cloned.1.call-start = ((), (), s32[]{:S(2)}) async-start(), calls=%async_computation.1 | async-start | bytes 4325376 | tf_op jit(solution)/shard_map/all_gather | solution.py:104
  11.6 5.3 %copy-start.7 = (s32[32,32]{1,0:T(8,128)S(1)}, s32[32,32]{1,0:T(8,128)}, u32[]{:S(2)}) copy-start(s32[32,32]{1,0:T(8,128)} %param.25) | copy-start | bytes 12292
  11.6 131.6 %all-gather.5.cloned.1.call-start = ((), (), s32[]{:S(2)}) async-start(), calls=%async_computation.2 | async-start | bytes 4325376 | tf_op jit(solution)/shard_map/all_gather | solution.py:105
  14.4 245.5 %all-reduce.5.cloned.1.call-start = ((), (), s32[]{:S(2)}) async-start(), calls=%async_computation.3 | async-start | bytes 2097152 | tf_op jit(solution)/shard_map/psum | solution.py:116
  208.2 3.6 copy-start.10
  208.4 64.7 %copy-start.8 = (s32[32]{0:T(128)S(1)}, s32[32]{0:T(128)}, u32[]{:S(2)}) copy-start(s32[32]{0:T(128)} %param.26) | copy-start | bytes 388
  211.8 68.8 %copy-start.5 = (bf16[512,1024]{1,0:T(8,128)(2,1)S(1)}, bf16[512,1024]{1,0:T(8,128)(2,1)}, u32[]{:S(2)}) copy-start(bf16[512,1024]{1,0:T(8,128)(2,1)} %param.28) | copy-start | bytes 3145732
  261.0 12.0 %copy-start.6 = (bf16[256,512]{1,0:T(8,128)(2,1)}, bf16[256,512]{1,0:T(8,128)(2,1)S(1)}, u32[]{:S(2)}) copy-start(bf16[256,512]{1,0:T(8,128)(2,1)S(1)} %add_convert_fusion.1) | copy-start | bytes 786436
  263.6 17.0 %all-to-all-start = ((bf16[32,2,256]{2,1,0:T(2,128)(2,1)}), bf16[32,2,256]{2,1,0:T(2,128)(2,1)S(1)}, u32[]{:S(2)}, u32[]{:S(2)}) async-start(bf16[32,2,256]{2,1,0:T(2,128)(2,1)} %reshape.196), calls=%async_computation | async-start | bytes 65536 | tf_op jit(solution)/shard_map/all_to_all | solution.py:128
  273.0 48.9 %all-reduce.7.cloned.1.call-start = ((), (), s32[]{:S(2)}) async-start(), calls=%async_computation.4 | async-start | bytes 131072 | tf_op jit(solution)/shard_map/psum | solution.py:132
  281.5 137.7 %all-reduce.9.cloned.1.call-start = ((), (), s32[]{:S(2)}) async-start(), calls=%async_computation.5 | async-start | bytes 4194304 | tf_op jit(solution)/shard_map/psum | solution.py:188
  322.8 6.1 %copy-start.9 = (bf16[1024,256]{1,0:T(8,128)(2,1)S(1)}, bf16[1024,256]{1,0:T(8,128)(2,1)}, u32[]{:S(2)}) copy-start(bf16[1024,256]{1,0:T(8,128)(2,1)} %param.32) | copy-start | bytes 1572868
  327.5 1.3 copy-start.2
  330.0 6.1 %copy-start.3 = (bf16[32,32,1024]{2,1,0:T(8,128)(2,1)S(1)}, bf16[32,32,1024]{2,1,0:T(8,128)(2,1)}, u32[]{:S(2)}) copy-start(bf16[32,32,1024]{2,1,0:T(8,128)(2,1)} %copy-done.2) | copy-start | bytes 6291460
  348.1 74.5 %copy-start.1 = (bf16[1024,1024]{1,0:T(8,128)(2,1)S(1)}, bf16[1024,1024]{1,0:T(8,128)(2,1)}, u32[]{:S(2)}) copy-start(bf16[1024,1024]{1,0:T(8,128)(2,1)} %param.29) | copy-start | bytes 6291460
Sparse Core Ops, SparseCore 0:
  11.8 67.1 all-gather.2
  81.3 61.8 all-gather.4
  211.9 47.9 all-reduce.4
  281.7 40.1 all-reduce.6
  353.0 66.2 all-reduce.8
where the time goes:
time: 430 us; the launch traced here: 429 us
  waiting for transfers between devices  276 us (64%)
  matrix products  63.6 us (15%)
  local copies, waits for them, and re-layouts  32.7 us (8%)
  other arithmetic  32.6 us (8%)
  between operations  14.1 us (3%)
  starting transfers between devices  9.67 us (2%)
    psum x1, waiting for transfers between devices, body(): lax.psum(depth_part.astype(jnp.bfloat16), 'tp').astype(jnp.float32)  66.4 us
    all_gather x1, waiting for transfers between devices, body(): lax.all_gather(values_local, 'seq', axis=0, tiled=True)  64.3 us
    all_gather x1, waiting for transfers between devices, body(): lax.all_gather(keys_local, 'seq', axis=0, tiled=True)  53.7 us
    psum x1, waiting for transfers between devices, body(): lax.psum(partial_out.astype(jnp.bfloat16), 'tp').astype(jnp.float32)  46.2 us
    psum x1, waiting for transfers between devices, body(): context = lax.psum(context_part.astype(jnp.bfloat16), 'tp')  40.3 us
    dot_general x1, matrix products, fold_piece(): jnp.einsum('cgqk,kcd->cgqd', weights.astype(jnp.bfloat16), values_piece,...  18.8 us
    dot_general x1, matrix products, fold_piece(): jnp.einsum('qcgd,kcd->cgqk', queries_grouped, keys_piece, preferred_eleme...  15.8 us
    reduce_sum x1, other arithmetic, fold_piece(): total_new = total_old * factor + jnp.sum(weights, axis=-1)  15 us
  transfers between devices with their start and end apart: 6, of which 6 were waited for; matrix products, arithmetic and copies ran while one was open for 4% of the time, Pallas kernels for 0%

commit v1 on v0

v1 whole, which is shorter than its diff:
```python
import functools
import math

import jax
import jax.numpy as jnp
from jax import lax
from jax.experimental import pallas as pl
from jax.experimental.pallas import tpu as pltpu
from jax.sharding import PartitionSpec as P

MESH = pl.DeviceIdType.MESH
BF16 = jnp.bfloat16
F32 = jnp.float32
LOG2E = math.log2(math.e)

ROWS = 256
D = 2048
HEAD = 128
DD = 1024
DHEAD = 64
LEVELS = 32
SEQ = 32
TP = 4
CHIPS = 16
PAIR = 2 * ROWS
QROWS = 8
DROWS = QROWS * LEVELS
NEG = -1e30

EVENTS = (
    ((0, 0), (0, 1), (1, 0), (0, 2), (1, 1), (0, 3)),
    ((1, 0), (1, 1), (0, 0), (1, 2), (0, 1), (1, 3), (0, 2), (0, 3)),
    ((2, 0), (2, 1), (1, 0), (2, 2), (1, 1), (0, 0), (2, 3), (1, 2), (1, 3), (0, 1), (0, 2), (0, 3)),
    (
        (3, 0), (2, 0), (0, 0), (3, 1), (2, 1), (1, 0), (3, 2), (2, 2),
        (0, 1), (3, 3), (2, 3), (1, 1), (0, 2), (1, 2), (0, 3), (1, 3),
    ),
)
ORDER = ((0, 1, 2, 3), (1, 0, 2, 3), (2, 1, 3, 0), (3, 2, 1, 0))
LEFT, RIGHT, UP, DOWN = range(4)


def pick(index, values):
    out = jnp.int32(values[0])
    for place, value in enumerate(values[1:], 1):
        out = jnp.where(index == place, jnp.int32(value), out)
    return out


def dot(a, b):
    return jnp.dot(a, b, preferred_element_type=F32)


def dot_nt(a, b):
    return lax.dot_general(a, b, (((1,), (1,)), ((), ())), preferred_element_type=F32)


def dot_tn(a, b):
    return lax.dot_general(a, b, (((0,), (0,)), ((), ())), preferred_element_type=F32)


def kernel(
    frames_h, wq_h, wk_h, wv_h, wo_h, pick_ref, codes_ref, geo_ref, geot_ref, wc_h, codet_h, level_ref,
    wdq_h, wdk_h, wdv_h, wdo_h,
    temporal_h, depth_h,
    frames, normed, wqkv, st, q_all, kv, m_s, l_s, acc_s, att_st, att_all, wo, temporal, wc, ctx_st, ctx_rv,
    codet, wall, wdo, hid, dn, datt, osend,
    load_sem, d2d_send, d2d_recv, kv_send, kv_recv, wo_send, wo_recv, wd_send, wd_recv, att_send, att_recv,
    ctx_send, ctx_recv, out_send, out_recv, self_sem,
):
    s = lax.axis_index("seq")
    t = lax.axis_index("tp")
    y = s // 8
    z = (s // 2) % 4
    c = s % 2
    chip = s // 2
    sib = s + 1 - 2 * c
    tn = (t + 1) % TP
    tb = (t + 3) % TP
    topp = (t + 2) % TP
    half = pl.multiple_of(c * ROWS, ROWS)

    def remote(src, dst, ssem, rsem, seq=None, tp=None):
        return pltpu.make_async_remote_copy(
            src_ref=src, dst_ref=dst, send_sem=ssem, recv_sem=rsem,
            device_id={"seq": s if seq is None else seq, "tp": t if tp is None else tp},
            device_id_type=MESH,
        )

    def cols(ref, start, size):
        return ref.at[:, pl.ds(pl.multiple_of(start * size, size), size)]

    loads = [
        pltpu.make_async_copy(frames_h, frames, load_sem.at[0]),
        pltpu.make_async_copy(wk_h, wqkv.at[:, 0:256], load_sem.at[1]),
        pltpu.make_async_copy(wv_h, wqkv.at[:, 256:512], load_sem.at[2]),
        pltpu.make_async_copy(wq_h, wqkv.at[:, 512:1024], load_sem.at[3]),
        pltpu.make_async_copy(wdq_h, wall.at[t, 0], load_sem.at[4]),
        pltpu.make_async_copy(wdk_h, wall.at[t, 1], load_sem.at[5]),
        pltpu.make_async_copy(wdv_h, wall.at[t, 2], load_sem.at[6]),
        pltpu.make_async_copy(wdo_h, wdo.at[pl.ds(pl.multiple_of(t * 256, 256), 256), :], load_sem.at[7]),
        pltpu.make_async_copy(
            cols(wo_h, t, 512), wo.at[pl.ds(pl.multiple_of(t * 512, 512), 512), :], load_sem.at[8]
        ),
        pltpu.make_async_copy(wc_h, wc, load_sem.at[9]),
        pltpu.make_async_copy(codet_h, codet, load_sem.at[10]),
    ]
    for load in loads:
        load.start()

    barrier = pltpu.get_barrier_semaphore()

    def greet(seq, tp):
        pl.semaphore_signal(barrier, inc=1, device_id={"seq": seq, "tp": tp}, device_id_type=MESH)

    seq_of = (s - 2, s + 2, ((y + 1) % 4) * 8 + s % 8, ((y + 3) % 4) * 8 + s % 8)
    greet(sib, t)
    greet(seq_of[UP], t)
    greet(seq_of[DOWN], t)

    @pl.when(z > 0)
    def _():
        greet(seq_of[LEFT], t)

    @pl.when(z < 3)
    def _():
        greet(seq_of[RIGHT], t)

    for tp in (tn, tb):
        greet(s, tp)
        greet(sib, tp)
    greet(s, topp)

    def greet_source(n, carry):
        src_seq, src_tp = t * 8 + n // TP, n % TP

        @pl.when(jnp.logical_not(jnp.logical_and(src_seq == s, src_tp == t)))
        def _():
            greet(src_seq, src_tp)

        return carry

    lax.fori_loop(0, 32, greet_source, 0)

    loads[0].wait()
    for r in range(4):
        rows = pl.ds(r * 64, 64)
        x = frames[rows, :].astype(F32)
        normed[rows, :] = (x * lax.rsqrt(jnp.mean(x * x, axis=-1, keepdims=True) + 1e-05)).astype(BF16)
    loads[1].wait()
    st[:, 0:256] = dot(normed[...], wqkv[:, 0:256]).astype(BF16)
    loads[2].wait()
    st[:, 256:512] = dot(normed[...], wqkv[:, 256:512]).astype(BF16)

    ends = jnp.where(z > 0, 1, 0) + jnp.where(z < 3, 1, 0)
    own_part = jnp.where(s // 8 == t, 1, 0)
    pl.semaphore_wait(barrier, 3 + ends + 5 + 32 - own_part)

    oc = 1 - c

    def lanes(start, size):
        return pl.ds(pl.multiple_of(start * size, size), size)

    my_rows = pl.ds(half, ROWS)
    d2d = [
        remote(st.at[:, lanes(oc, 128)], kv.at[chip, my_rows, 0:128], d2d_send.at[0], d2d_recv.at[0], seq=sib),
        remote(st.at[:, lanes(2 + oc, 128)], kv.at[chip, my_rows, 128:256], d2d_send.at[1], d2d_recv.at[1], seq=sib),
        remote(st.at[:, lanes(2 + oc, 256)], q_all.at[my_rows, :], d2d_send.at[2], d2d_recv.at[2], seq=sib),
    ]
    d2d[0].start()
    d2d[1].start()
    kv[chip, my_rows, 0:128] = st[:, lanes(c, 128)]
    kv[chip, my_rows, 128:256] = st[:, lanes(2 + c, 128)]

    wo_half = pl.multiple_of(c * 256, 256)

    def wo_rows(tp, core):
        return wo.at[pl.ds(pl.multiple_of(tp * 512 + core * 256, 256), 256), :]

    wo_copies = []
    for n, tp in enumerate((topp, tn, tb)):
        wo_copies.append(
            remote(
                wo_h.at[pl.ds(wo_half, 256), pl.ds(pl.multiple_of(tp * 512, 512), 512)],
                wo_rows(t, c), wo_send.at[n], wo_recv.at[t], tp=tp,
            )
        )
    loads[3].wait()
    st[:, 512:768] = dot(normed[...], wqkv[:, 512:768]).astype(BF16)
    st[:, 768:1024] = dot(normed[...], wqkv[:, 768:1024]).astype(BF16)
    d2d[2].start()
    q_all[my_rows, :] = st[:, lanes(2 + c, 256)]

    def event(e, here):
        if not isinstance(e, int):
            codes = []
            for row in range(4):
                listed = [br * 4 + k for br, k in EVENTS[row]]
                codes.append(pick(e, listed + [-1] * (16 - len(listed))))
            code = jnp.where(y == 0, codes[0], jnp.where(y == 1, codes[1], jnp.where(y == 2, codes[2], codes[3])))
        else:
            code = y * 4
        present = code >= 0
        code = jnp.maximum(code, 0)
        br = code // 4
        k = code % 4
        bz = pick(k, (0, 0, 0, 0))
        for zz in range(4):
            bz = jnp.where(z == zz, pick(k, ORDER[zz]), bz)
        valid = jnp.logical_and(present, jnp.logical_or(br < 3, bz <= z))
        row = br == y
        both = lambda *conds: functools.reduce(jnp.logical_and, conds)
        either = lambda *conds: functools.reduce(jnp.logical_or, conds)
        left = both(valid, row, z > 0, bz >= z, y < 3)
        right = both(valid, row, z < 3, bz <= z)
        up = both(
            valid,
            either(both(row, y < 3), both(y == 1, br == 0, k >= 2), both(y == 2, br == 1, k >= 2)),
        )
        down = both(
            valid,
            either(
                both(row, either(y == 0, both(y == 1, k < 2))),
                both(y == 0, br == 1),
                both(y == 3, br == 0, k < 2),
            ),
        )
        used = both(valid, either(br < y, both(row, bz < z)))
        return br * 4 + bz, valid, used, (left, right, up, down)

    def kv_copy(b, way):
        return remote(kv.at[b], kv.at[b], kv_send.at[way, b], kv_recv.at[b], seq=seq_of[way])

    def forward(b, ways):
        for way in (UP, DOWN, RIGHT, LEFT):
            @pl.when(ways[way])
            def _():
                kv_copy(b, way).start()

    scale = HEAD ** (-0.5) * LOG2E

    def fold(b, first):
        for h in range(2):
            keys = kv[b, :, 0:128]
            values = kv[b, :, 128:256]
            scores = dot_nt(keys, q_all[:, h * 128 : (h + 1) * 128])
            if first:
                kpos = lax.broadcasted_iota(jnp.int32, (PAIR, PAIR), 0)
                qpos = lax.broadcasted_iota(jnp.int32, (PAIR, PAIR), 1)
                scores = jnp.where(kpos <= qpos, scores, NEG)
                top = jnp.max(scores, axis=0, keepdims=True)
                weights = jnp.exp2((scores - top) * scale)
                l_s[h] = jnp.sum(weights, axis=0, keepdims=True)
                acc_s[h] = dot_tn(values, weights.astype(BF16))
                m_s[h] = top
            else:
                old = m_s[h]
                top = jnp.maximum(old, jnp.max(scores, axis=0, keepdims=True))
                weights = jnp.exp2((scores - top) * scale)
                factor = jnp.exp2((old - top) * scale)
                l_s[h] = l_s[h] * factor + jnp.sum(weights, axis=0, keepdims=True)
                acc_s[h] = acc_s[h] * factor + dot_tn(values, weights.astype(BF16))
                m_s[h] = top

    d2d[0].wait_recv()
    d2d[1].wait_recv()
    first_block, _, _, first_ways = event(0, True)
    forward(first_block, first_ways)

    for copy in wo_copies:
        copy.start()

    def qkv_part(tp, lo, n):
        return wall.at[tp, :, pl.ds(pl.multiple_of(lo * 4, 256), n * 4), :]

    def out_part(tp, lo, n):
        return wdo.at[pl.ds(pl.multiple_of(tp * 256 + lo, 64), n), :]

    parts = (qkv_part, out_part)
    mine = c * 128
    theirs = oc * 128

    def wd_direct(p, tp):
        ref = parts[p](t, mine, 128)
        return remote(ref, ref, wd_send.at[p, 0 if tp is tn else 1], wd_recv.at[p, 0 if tp is tn else 1], tp=tp)

    for load in loads[4:8]:
        load.wait()
    for p in range(2):
        for tp in (tn, tb):
            wd_direct(p, tp).start()

    def wd_relay(p, way):
        tp = (tb, tn)[way]
        ref = parts[p](tp, mine + way * 64, 64)
        return remote(ref, ref, wd_send.at[p, 2 + way], wd_recv.at[p, 2 + way], tp=(tn, tb)[way])

    def wd_hand(p, way, core_lo):
        tp = (tb, tn)[way]
        ref = parts[p](tp, core_lo, 128)
        return remote(ref, ref, wd_send.at[p, 4 + way], wd_recv.at[p, 4 + way], seq=sib)

    def wd_hand_relayed(p, way, core_lo):
        ref = parts[p](topp, core_lo + way * 64, 64)
        return remote(ref, ref, wd_send.at[p, 6 + way], wd_recv.at[p, 6 + way], seq=sib)

    def wd_direct_arrived(p, way):
        ref = parts[p]((tb, tn)[way], mine, 128)
        return remote(ref, ref, wd_send.at[p, way], wd_recv.at[p, way], tp=(tn, tb)[way])

    def wd_relay_arrived(p, way):
        ref = parts[p](topp, mine + way * 64, 64)
        return remote(ref, ref, wd_send.at[p, 2 + way], wd_recv.at[p, 2 + way], tp=(tn, tb)[way])

    def wd_pass(p):
        for way in range(2):
            wd_direct_arrived(p, way).wait_recv()
            wd_relay(p, way).start()
            wd_hand(p, way, mine).start()

    def wo_arrived(tp, core, slot):
        ref = wo_rows(tp, core)
        return remote(ref, ref, wo_send.at[0], wo_recv.at[slot], seq=sib)

    d2d[2].wait_recv()
    fold(first_block, True)

    def step(e, carry):
        b, valid, used, ways = event(e, False)

        @pl.when(valid)
        def _():
            kv_copy(b, UP).wait_recv()
            forward(b, ways)

        @pl.when(used)
        def _():
            fold(b, False)

        @pl.when(e == 10)
        def _():
            for n, tp in enumerate((topp, tn, tb)):
                remote(wo_rows(tp, c), wo_rows(tp, c), wo_send.at[n], wo_recv.at[tp], seq=sib).wait_recv()
                remote(wo_rows(tp, c), wo_rows(tp, c), wo_send.at[3 + n], wo_recv.at[4 + tp], seq=sib).start()
            wd_pass(0)

        @pl.when(e == 12)
        def _():
            wd_pass(1)

        return carry

    lax.fori_loop(1, 16, step, 0)

    for h in range(2):
        heads = acc_s[h] / l_s[h]
        heads = heads * lax.rsqrt(jnp.mean(heads * heads, axis=0, keepdims=True) + 1e-06)
        att_st[:, h * 128 : (h + 1) * 128] = heads.T.astype(BF16)

    def att_copy(core, slot, seq, tp):
        return remote(
            att_st.at[pl.ds(pl.multiple_of(core * ROWS, ROWS), ROWS), :], att_all.at[t * 2 + c],
            att_send.at[slot], att_recv.at[t * 2 + c], seq=seq, tp=tp,
        )

    att_copies = [
        att_copy(c, 0, s, tn), att_copy(c, 1, s, tb), att_copy(oc, 2, sib, tn), att_copy(oc, 3, sib, tb),
        att_copy(oc, 4, sib, t),
    ]
    for copy in att_copies:
        copy.start()
    att_all[t * 2 + c] = att_st[my_rows, :]

    loads[10].wait()
    row_level = lax.broadcasted_iota(jnp.int32, (DROWS, LEVELS), 0) % LEVELS
    lane = lax.broadcasted_iota(jnp.int32, (DROWS, LEVELS), 1)
    my_codes = codes_ref[pl.ds(pl.multiple_of(t * QROWS, QROWS), QROWS), :]
    spread = jnp.broadcast_to(my_codes[:, None, :], (QROWS, LEVELS, LEVELS)).reshape(DROWS, LEVELS)
    code = jnp.sum(jnp.where(lane == row_level - 1, spread, 0), axis=-1, keepdims=True)
    level0 = lax.broadcasted_iota(jnp.int32, (DROWS, 1), 0) % LEVELS == 0
    code = jnp.where(level0, -1, code)
    slab_row = lax.broadcasted_iota(jnp.int32, (DROWS, LEVELS), 0) // LEVELS + t * QROWS
    geo = jnp.sum(jnp.where(lane == slab_row, jnp.broadcast_to(geo_ref[...], (DROWS, LEVELS)), 0), axis=-1, keepdims=True)
    code_hot = (lax.broadcasted_iota(jnp.int32, (DROWS, DD), 1) == code).astype(F32).astype(BF16)
    geo_hot = (lax.broadcasted_iota(jnp.int32, (DROWS, 64), 1) == geo).astype(F32).astype(BF16)
    for n in range(4):
        part = slice(n * 256, (n + 1) * 256)
        level = jnp.broadcast_to(level_ref[:, part].astype(F32)[None], (QROWS, LEVELS, 256)).reshape(DROWS, 256)
        hid[:, part] = dot(code_hot, codet[:, part]) + dot(geo_hot, geot_ref[:, part]) + level

    def att_arrived(tp, core):
        ref = att_all.at[tp * 2 + core]
        return remote(ref, ref, att_send.at[0], att_recv.at[tp * 2 + core], seq=sib)

    def att_relay(tp, core, slot, to):
        ref = att_all.at[tp * 2 + core]
        return remote(ref, ref, att_send.at[slot], att_recv.at[tp * 2 + core], tp=to)

    loads[8].wait()
    for n, tp in enumerate((topp, tn, tb)):
        wo_arrived(tp, oc, 4 + tp).wait_recv()

    def project(tp, core):
        rows = pl.ds(pl.multiple_of(tp * 512 + core * 256, 256), 256)
        return dot(att_all[tp * 2 + core], wo[rows, :])

    total = frames[:, pl.ds(pl.multiple_of(t * 512, 512), 512)].astype(F32) + project(t, c)
    att_arrived(t, oc).wait_recv()
    total += project(t, oc)
    relays = [att_relay(tb, 0, 5, tn), att_relay(tn, 1, 6, tb)]
    att_arrived(tb, 0).wait_recv()
    relays[0].start()
    att_arrived(tn, 1).wait_recv()
    relays[1].start()
    total += project(tb, 0) + project(tn, 1)
    for tp, core in ((tb, 1), (tn, 0), (topp, 0), (topp, 1)):
        att_arrived(tp, core).wait_recv()
        total += project(tp, core)
    temporal[...] = total.astype(BF16)
    write = pltpu.make_async_copy(temporal, temporal_h, load_sem.at[11])
    write.start()

    loads[9].wait()
    pick_hot = (lax.broadcasted_iota(jnp.int32, (SEQ, ROWS), 1) == pick_ref[...]).astype(F32).astype(BF16)
    picked = dot(pick_hot, temporal[...]).astype(BF16)
    for n in range(8):
        ctx_st[:, n, :] = dot(picked, wc[:, n * 128 : (n + 1) * 128])
    to_tp = s // 8
    slot = (s % 8) * TP + t

    def ctx_copy(j):
        return remote(
            ctx_st.at[j], ctx_rv.at[slot], ctx_send.at[j], ctx_recv.at[slot], seq=j, tp=to_tp
        )

    own_ctx = pltpu.make_async_copy(ctx_st.at[s], ctx_rv.at[slot], self_sem)
    stays = to_tp == t

    def ctx_out(j, carry):
        @pl.when(jnp.logical_not(jnp.logical_and(j == s, stays)))
        def _():
            ctx_copy(j).start()

        return carry

    lax.fori_loop(0, SEQ, ctx_out, 0)

    @pl.when(stays)
    def _():
        own_ctx.start()
        own_ctx.wait()

    for p in range(2):
        for way in range(2):
            wd_relay_arrived(p, way).wait_recv()
            wd_hand_relayed(p, way, mine).start()

    def ctx_in(n, carry):
        @pl.when(jnp.logical_not(jnp.logical_and(n == slot, stays)))
        def _():
            ref = ctx_rv.at[n]
            remote(ref, ref, ctx_send.at[n], ctx_recv.at[n], seq=sib).wait_recv()

        return carry

    lax.fori_loop(0, SEQ, ctx_in, 0)

    square = jnp.zeros((DROWS, 1), F32)
    for n in range(8):
        part = slice(n * 128, (n + 1) * 128)
        rows = []
        for r in range(QROWS):
            row = ctx_rv[r * TP, n : n + 1, :]
            for tp in range(1, TP):
                row = row + ctx_rv[r * TP + tp, n : n + 1, :]
            rows.append(jnp.broadcast_to(row.astype(BF16).astype(F32), (LEVELS, 128)))
        value = hid[:, part] + jnp.concatenate(rows, axis=0)
        hid[:, part] = value
        square += jnp.sum(value * value, axis=-1, keepdims=True)
    factor = lax.rsqrt(square * (1.0 / DD) + 1e-05)
    dn[...] = (hid[...] * factor).astype(BF16)

    for p in range(2):
        for way in range(2):
            wd_hand(p, way, theirs).wait_recv()
            wd_hand_relayed(p, way, theirs).wait_recv()

    dscale = DHEAD ** (-0.5) * LOG2E
    lrow = lax.broadcasted_iota(jnp.int32, (128, 128), 0)
    lcol = lax.broadcasted_iota(jnp.int32, (128, 128), 1)
    allowed = jnp.logical_and(lrow // LEVELS == lcol // LEVELS, lcol <= lrow)

    def depth_heads(g, carry):
        queries = dot(dn[...], wall[g, 0]).astype(BF16)
        keys = dot(dn[...], wall[g, 1]).astype(BF16)
        values = dot(dn[...], wall[g, 2]).astype(BF16)
        outs = []
        for r in range(2):
            rows = slice(r * 128, (r + 1) * 128)
            parts_out = []
            for h in range(4):
                part = slice(h * DHEAD, (h + 1) * DHEAD)
                scores = dot_nt(queries[rows, part], keys[rows, part])
                scores = jnp.where(allowed, scores, NEG)
                top = jnp.max(scores, axis=-1, keepdims=True)
                weights = jnp.exp2((scores - top) * dscale)
                sums = jnp.sum(weights, axis=-1, keepdims=True)
                heads = dot(weights.astype(BF16), values[rows, part]) / sums
                heads = heads * lax.rsqrt(jnp.mean(heads * heads, axis=-1, keepdims=True) + 1e-06)
                parts_out.append(heads.astype(BF16))
            outs.append(jnp.concatenate(parts_out, axis=1))
        datt[:, pl.ds(pl.multiple_of(g * 256, 256), 256)] = jnp.concatenate(outs, axis=0)
        return carry

    lax.fori_loop(0, TP, depth_heads, 0)

    def out_tile(tp):
        part = pl.ds(pl.multiple_of(tp * 256, 256), 256)
        return (dot(datt[...], wdo[:, part]) + hid[:, part]).astype(BF16)

    def out_rows(tp):
        return depth_h.at[pl.ds(pl.multiple_of(tp * DROWS, DROWS), DROWS), :]

    out_copies = []
    for n, tp in enumerate((topp, tn, tb)):
        osend[n] = out_tile(tp)
        copy = remote(osend.at[n], out_rows(t), out_send.at[n], out_recv.at[t], tp=tp)
        copy.start()
        out_copies.append(copy)
    osend[3] = out_tile(t)
    own_out = pltpu.make_async_copy(osend.at[3], out_rows(t), load_sem.at[12])
    own_out.start()

    for copy in d2d + wo_copies + att_copies + relays:
        copy.wait_send()
    for n, tp in enumerate((topp, tn, tb)):
        remote(wo_rows(tp, c), wo_rows(tp, c), wo_send.at[3 + n], wo_recv.at[4 + tp], seq=sib).wait_send()
    for p in range(2):
        for tp in (tn, tb):
            wd_direct(p, tp).wait_send()
        for way in range(2):
            wd_relay(p, way).wait_send()
            wd_hand(p, way, mine).wait_send()
            wd_hand_relayed(p, way, mine).wait_send()

    def sent(e, carry):
        b, _, _, ways = event(e, False)
        for way in range(4):
            @pl.when(ways[way])
            def _():
                kv_copy(b, way).wait_send()

        return carry

    for way in range(4):
        @pl.when(first_ways[way])
        def _():
            kv_copy(first_block, way).wait_send()

    lax.fori_loop(1, 16, sent, 0)

    def ctx_sent(j, carry):
        @pl.when(jnp.logical_not(jnp.logical_and(j == s, stays)))
        def _():
            ctx_copy(j).wait_send()

        return carry

    lax.fori_loop(0, SEQ, ctx_sent, 0)
    write.wait()
    own_out.wait()
    for n, tp in enumerate((topp, tn, tb)):
        out_copies[n].wait_send()
    for tp in (topp, tn, tb):
        remote(osend.at[0], out_rows(tp), out_send.at[0], out_recv.at[tp], tp=tp).wait_recv()


def body(
    frames, w_query, w_key, w_value, w_out, frame_pick, codes, geo_ids, geo_table, w_context, code_table,
    level_table, wd_query, wd_key, wd_value, wd_out,
):
    hbm = pl.BlockSpec(memory_space=pl.ANY)
    vmem = pl.BlockSpec(memory_space=pltpu.VMEM)
    sem = pltpu.SemaphoreType.DMA
    temporal, depth = pl.pallas_call(
        kernel,
        out_shape=(
            jax.ShapeDtypeStruct((ROWS, 512), BF16),
            jax.ShapeDtypeStruct((SEQ * LEVELS, 256), BF16),
        ),
        in_specs=[hbm, hbm, hbm, hbm, hbm, vmem, vmem, vmem, vmem, hbm, hbm, vmem, hbm, hbm, hbm, hbm],
        out_specs=(hbm, hbm),
        scratch_shapes=[
            pltpu.VMEM((ROWS, D), BF16),
            pltpu.VMEM((ROWS, D), BF16),
            pltpu.VMEM((D, 1024), BF16),
            pltpu.VMEM((ROWS, 1024), BF16),
            pltpu.VMEM((PAIR, 256), BF16),
            pltpu.VMEM((CHIPS, PAIR, 256), BF16),
            pltpu.VMEM((2, 1, PAIR), F32),
            pltpu.VMEM((2, 1, PAIR), F32),
            pltpu.VMEM((2, HEAD, PAIR), F32),
            pltpu.VMEM((PAIR, 256), BF16),
            pltpu.VMEM((TP * 2, ROWS, 256), BF16),
            pltpu.VMEM((D, 512), BF16),
            pltpu.VMEM((ROWS, 512), BF16),
            pltpu.VMEM((512, DD), BF16),
            pltpu.VMEM((SEQ, 8, 128), F32),
            pltpu.VMEM((SEQ, 8, 128), F32),
            pltpu.VMEM((DD, DD), BF16),
            pltpu.VMEM((TP, 3, DD, 256), BF16),
            pltpu.VMEM((DD, DD), BF16),
            pltpu.VMEM((DROWS, DD), F32),
            pltpu.VMEM((DROWS, DD), BF16),
            pltpu.VMEM((DROWS, DD), BF16),
            pltpu.VMEM((TP, DROWS, 256), BF16),
            sem((13,)),
            sem((3,)),
            sem((3,)),
            sem((4, CHIPS)),
            sem((CHIPS,)),
            sem((6,)),
            sem((8,)),
            sem((2, 8)),
            sem((2, 8)),
            sem((7,)),
            sem((8,)),
            sem((SEQ,)),
            sem((SEQ,)),
            sem((3,)),
            sem((TP,)),
            sem(()),
        ],
        compiler_params=pltpu.CompilerParams(
            collective_id=0, has_side_effects=True, vmem_limit_bytes=58 * 1024 * 1024
        ),
        name="codec_layers",
    )(
        frames, w_query, w_key, w_value, w_out, frame_pick.reshape(SEQ, 1), codes, geo_ids.reshape(1, SEQ),
        geo_table, w_context, code_table, level_table, wd_query, wd_key, wd_value, wd_out,
    )
    return temporal, depth.reshape(SEQ, LEVELS, 256)


def solution(mesh):
    return jax.shard_map(
        body,
        mesh=mesh,
        in_specs=(
            P(("dp", "seq"), None),
            P(None, "tp"),
            P(None, "tp"),
            P(None, "tp"),
            P("tp", None),
            P(("dp", "seq"), None, None),
            P(("dp", "seq"), None),
            P(("dp", "seq")),
            P(),
            P("tp", None),
            P(),
            P(),
            P(None, "tp"),
            P(None, "tp"),
            P(None, "tp"),
            P("tp", None),
        ),
        out_specs=(P(("dp", "seq"), "tp"), P(("dp", "seq"), None, "tp")),
        check_vma=False,
    )
```

time: 430 us -> 106 us (0.25)
  waiting for transfers between devices: 276 us -> 0 us
  Pallas kernels: 0 us -> 99.8 us
  matrix products: 63.6 us -> 0 us
  other arithmetic: 32.6 us -> 0 us
  local copies, waits for them, and re-layouts: 32.7 us -> 4.88 us
  between operations: 14.1 us -> 0.64 us
  starting transfers between devices: 9.67 us -> 0 us
    psum x3 -> x0, waiting for transfers between devices: 153 us -> none  [the longest x1 66.4 us: body(): lax.psum(depth_part.astype(jnp.bfloat16), 'tp').astype(jnp.float32)]
    all_gather x2 -> x0, waiting for transfers between devices: 118 us -> none  [the longest x1 64.3 us: body(): lax.all_gather(values_local, 'seq', axis=0, tiled=True)]
    pallas_call x0 -> x1, Pallas kernels: none -> 99.8 us  [body(): pl.pallas_call(kernel, out_shape=(jax.ShapeDtypeStruct((ROWS, 512), BF16)...]
    dot_general x13 -> x0, matrix products: 60.2 us -> none  [the longest x1 18.8 us: fold_piece(): jnp.einsum('cgqk,kcd->cgqd', weights.astype(jnp.bfloat16), values_piece,...]
    reshape x7 -> x1, local copies, waits for them, and re-layouts: 20.5 us -> 1.34 us  [body(): frame_pick.reshape(SEQ, 1)]
    reduce_sum x3 -> x0, other arithmetic: 16.8 us -> none  [the longest x1 15 us: fold_piece(): total_new = total_old * factor + jnp.sum(weights, axis=-1)]
    all_to_all x1 -> x0, starting transfers between devices: 9.46 us -> none  [body(): lax.all_to_all(chosen, 'seq', split_axis=0, concat_axis=0, tiled=True)]
    gather x3 -> x0, local copies, waits for them, and re-layouts: 8.84 us -> none  [the longest x2 8.21 us: body(): code_rows = jnp.take(code_table, codes[:, :-1], axis=0).astype(jnp.float32)]
  transfers between devices with their start and end apart: 6 -> 0, of which waited for: 6 -> 0; matrix products, arithmetic and copies ran while one was open for 4% -> 0% of each run, Pallas kernels for 0% -> 0%
where the time goes in v1:
time: 106 us; the launch traced here: 105 us
  Pallas kernels  99.8 us (94%)
  local copies, waits for them, and re-layouts  4.88 us (5%)
    pallas_call x1, Pallas kernels, body(): pl.pallas_call(kernel, out_shape=(jax.ShapeDtypeStruct((ROWS, 512), BF16)...  99.8 us
    unnamed x2, local copies, waits for them, and re-layouts  3.54 us

profile of v1, /device:TPU:1, one launch (start us, length us, event | category | flops | bytes accessed | tf_op | source)
XLA Modules:
  0.0 105.3 jit_solution(1910999631808229068)
XLA Ops:
  0.6 1.3 %copy.18.pick_ref = s32[32,1]{1,0:T(8,128)} copy(s32[32,1]{0,1:T(1,128)} %bitcast.5) | data formatting | bytes 256 | tf_op jit(solution)/shard_map/reshape | solution.py:639
  2.0 99.8 %codec_layers.1 = (bf16[256,512]{1,0:T(8,128)(2,1)}, bf16[1024,256]{1,0:T(8,128)(2,1)}) custom-call(bf16[256,2048]{1,0:T(8,128)(2,1)} %frames_h.1, bf16[2048,512]{1,0:T(8,128)(2,1)} %wq_h.1, bf16[2048,256]{1,0:T(8,128)(2,1)} %wk_h.1, bf16[2048,256]{1,0:T(8,128)(2,1)} %wv_h.1, bf16[512,2048]{1,0:T(8,128)(2,1)} %wo_h.1, s32[32,1]{1,0:T(8,128)} %copy.18.pick_ref, ...), custom_call_target="tpu_custom_call" | custom-call | tf_op jit(solution)/shard_map/codec_layers/pallas_call | solution.py:585
  101.8 1.7 %copy.21 = bf16[256,512]{1,0:T(8,128)(2,1)} copy(bf16[256,512]{1,0:T(8,128)(2,1)} %get-tuple-element.8) | data formatting | bytes 524288
  103.5 1.9 %copy.22 = bf16[32,32,256]{2,1,0:T(8,128)(2,1)} copy(bf16[32,32,256]{2,1,0:T(8,128)(2,1)} %bitcast.3) | data formatting | bytes 1048576

commit v2 on v1

v2 whole, which is shorter than its diff:
```python
import functools
import math

import jax
import jax.numpy as jnp
from jax import lax
from jax.experimental import pallas as pl
from jax.experimental.pallas import tpu as pltpu
from jax.sharding import PartitionSpec as P

MESH = pl.DeviceIdType.MESH
BF16 = jnp.bfloat16
F32 = jnp.float32
LOG2E = math.log2(math.e)

ROWS = 256
D = 2048
HEAD = 128
DD = 1024
DHEAD = 64
LEVELS = 32
SEQ = 32
TP = 4
CHIPS = 16
PAIR = 2 * ROWS
QROWS = 8
DROWS = QROWS * LEVELS
NEG = -1e30

EVENTS = (
    ((0, 0), (0, 1), (1, 0), (1, 1), (0, 2), (0, 3)),
    ((1, 0), (1, 1), (0, 0), (0, 1), (1, 2), (0, 2), (1, 3), (0, 3)),
    ((2, 0), (2, 1), (1, 0), (0, 0), (1, 1), (0, 1), (2, 2), (1, 2), (0, 2), (2, 3), (1, 3), (0, 3)),
    (
        (3, 0), (3, 1), (2, 0), (0, 0), (2, 1), (0, 1), (1, 0), (3, 2),
        (2, 2), (1, 1), (1, 2), (0, 2), (3, 3), (2, 3), (0, 3), (1, 3),
    ),
)
ORDER = tuple(tuple(z ^ k for k in range(4)) for z in range(4))
ACROSS, UP, DOWN = range(3)


def event_fields(y, z, e):
    if e >= len(EVENTS[y]):
        return 0
    br, k = EVENTS[y][e]
    bz = ORDER[z][k]
    if br == 3 and bz // 2 > z // 2:
        return 0
    row = br == y
    across = row and k < 2 and (y < 3 or z < 2)
    up = (row and y < 3) or (y == 1 and br == 0 and k >= 2) or (y == 2 and br == 1 and k >= 2)
    down = (row and (y == 0 or (y == 1 and k < 2))) or (y == 0 and br == 1) or (y == 3 and br == 0 and k < 2)
    used = br < y or (row and bz // 2 <= z // 2)
    bits = br * 4 + bz
    for place, flag in enumerate((True, used, across, up, down)):
        bits += int(flag) << (4 + place)
    return bits


EVENT_WORDS = tuple(
    tuple(
        sum(event_fields(n // 4, n % 4, 3 * w + i) << (10 * i) for i in range(3)) for n in range(CHIPS)
    )
    for w in range(6)
)


def pick(index, values):
    out = jnp.int32(values[0]) if isinstance(values[0], int) else values[0]
    for place, value in enumerate(values[1:], 1):
        out = jnp.where(index == place, jnp.int32(value) if isinstance(value, int) else value, out)
    return out


def dot(a, b):
    return jnp.dot(a, b, preferred_element_type=F32)


def dot_nt(a, b):
    return lax.dot_general(a, b, (((1,), (1,)), ((), ())), preferred_element_type=F32)


def dot_tn(a, b):
    return lax.dot_general(a, b, (((0,), (0,)), ((), ())), preferred_element_type=F32)


def kernel(
    frames_h, wq_h, wk_h, wv_h, wo_h, pick_ref, codes_ref, geo_ref, geot_ref, wc_h, codet_h, level_ref,
    wdq_h, wdk_h, wdv_h, wdo_h,
    temporal_h, depth_h,
    frames, normed, wqkv, kv_st, q_st, q_all, kv, m_s, l_s, acc_s, att_st, att_all, wo, temporal, wc, ctx_st, ctx_in, ctx_mine, ctx_rv,
    codet, wall, wdo, hid, dn, datt, osend,
    load_sem, d2d_send, q_recv, kv_send, kv_recv, sib_send, sib_recv, wo_send, wo_recv, wd_send, wd_recv, att_send, att_recv,
    ctx_send, ctx_recv, row_send, row_recv, out_send, out_recv, self_sem,
):
    s = lax.axis_index("seq")
    t = lax.axis_index("tp")
    y = s // 8
    z = (s // 2) % 4
    c = s % 2
    chip = s // 2
    sib = s + 1 - 2 * c
    tn = (t + 1) % TP
    tb = (t + 3) % TP
    topp = (t + 2) % TP
    half = pl.multiple_of(c * ROWS, ROWS)

    def remote(src, dst, ssem, rsem, seq=None, tp=None):
        return pltpu.make_async_remote_copy(
            src_ref=src, dst_ref=dst, send_sem=ssem, recv_sem=rsem,
            device_id={"seq": s if seq is None else seq, "tp": t if tp is None else tp},
            device_id_type=MESH,
        )

    def cols(ref, start, size):
        return ref.at[:, pl.ds(pl.multiple_of(start * size, size), size)]

    loads = [
        pltpu.make_async_copy(frames_h, frames, load_sem.at[0]),
        pltpu.make_async_copy(wk_h, wqkv.at[:, 0:256], load_sem.at[1]),
        pltpu.make_async_copy(wv_h, wqkv.at[:, 256:512], load_sem.at[2]),
        pltpu.make_async_copy(wq_h, wqkv.at[:, 512:1024], load_sem.at[3]),
        pltpu.make_async_copy(wdq_h, wall.at[t, 0], load_sem.at[4]),
        pltpu.make_async_copy(wdk_h, wall.at[t, 1], load_sem.at[5]),
        pltpu.make_async_copy(wdv_h, wall.at[t, 2], load_sem.at[6]),
        pltpu.make_async_copy(wdo_h, wdo.at[pl.ds(pl.multiple_of(t * 256, 256), 256), :], load_sem.at[7]),
        pltpu.make_async_copy(
            cols(wo_h, t, 512), wo.at[pl.ds(pl.multiple_of(t * 512, 512), 512), :], load_sem.at[8]
        ),
        pltpu.make_async_copy(wc_h, wc, load_sem.at[9]),
        pltpu.make_async_copy(codet_h, codet, load_sem.at[10]),
    ]
    for load in loads:
        load.start()

    barrier = pltpu.get_barrier_semaphore()

    def greet(seq, tp):
        pl.semaphore_signal(barrier, inc=1, device_id={"seq": seq, "tp": tp}, device_id_type=MESH)

    p = z % 2
    op = 1 - p
    mate = s + 2 * (1 - 2 * p)
    mate_sib = sib + 2 * (1 - 2 * p)
    seq_of = (s + 4 * (1 - 2 * (z // 2)), ((y + 1) % 4) * 8 + s % 8, ((y + 3) % 4) * 8 + s % 8)
    greet(sib, t)
    greet(mate, t)
    greet(mate_sib, t)
    for way in range(3):
        greet(seq_of[way], t)
    for tp in (tn, tb):
        greet(s, tp)
        greet(sib, tp)
    greet(s, topp)

    for n in range(QROWS):
        @pl.when(jnp.logical_not(jnp.logical_and(t * 8 + n == s, s // 8 == t)))
        def _():
            greet(t * 8 + n, s // 8)

    loads[0].wait()
    for r in range(4):
        rows = pl.ds(r * 64, 64)
        x = frames[rows, :].astype(F32)
        normed[rows, :] = (x * lax.rsqrt(jnp.mean(x * x, axis=-1, keepdims=True) + 1e-05)).astype(BF16)
    loads[1].wait()
    both = dot(normed[...], wqkv[:, 0:256]).astype(BF16)
    kv_st[0, :, 0:128] = both[:, 0:128]
    kv_st[1, :, 0:128] = both[:, 128:256]
    loads[2].wait()
    both = dot(normed[...], wqkv[:, 256:512]).astype(BF16)
    kv_st[0, :, 128:256] = both[:, 0:128]
    kv_st[1, :, 128:256] = both[:, 128:256]

    own_part = jnp.where(s // 8 == t, 1, 0)
    pl.semaphore_wait(barrier, 6 + 5 + QROWS - own_part)

    oc = 1 - c
    my_rows = pl.ds(half, ROWS)
    other_rows = pl.ds(pl.multiple_of(oc * ROWS, ROWS), ROWS)

    def kv_half(b, rows):
        return kv.at[b, rows, :]

    kv_mate = remote(kv_st.at[op], kv_half(chip, my_rows), d2d_send.at[0], kv_recv.at[chip], seq=mate)
    kv_sib = remote(kv_st.at[p], kv_half(chip, my_rows), d2d_send.at[1], sib_recv.at[chip], seq=sib)
    kv_mate.start()
    kv_sib.start()
    kv[chip, my_rows, :] = kv_st[p]

    def kv_copy(b, way):
        return remote(kv_half(b, my_rows), kv_half(b, my_rows), kv_send.at[way, b], kv_recv.at[b], seq=seq_of[way])

    def sib_copy(b):
        return remote(kv_half(b, my_rows), kv_half(b, my_rows), sib_send.at[b], sib_recv.at[b], seq=sib)

    def forward(b, ways):
        for way in (DOWN, UP, ACROSS):
            @pl.when(ways[way])
            def _():
                kv_copy(b, way).start()

    words = [pick(chip, table) for table in EVENT_WORDS]

    def event(e):
        word = pick(e // 3, words)
        place = e % 3
        bits = jnp.where(place == 0, word, jnp.where(place == 1, word // 1024, word // (1024 * 1024)))
        flags = [(bits // (16 << n)) % 2 == 1 for n in range(5)]
        return bits % 16, flags[0], flags[1], flags[2:]

    first_block, _, _, first_ways = event(jnp.int32(0))
    forward(first_block, first_ways)

    q_slot = p * 2 + c

    def q_copy(n, seq, head):
        return remote(q_st.at[head], q_all.at[q_slot], d2d_send.at[2 + n], q_recv.at[q_slot], seq=seq)

    q_copies = [
        q_copy(0, mate, op * 2 + c), q_copy(1, mate_sib, op * 2 + oc), q_copy(2, sib, p * 2 + oc),
    ]

    wo_half = pl.multiple_of(c * 256, 256)

    def wo_rows(tp, core):
        return wo.at[pl.ds(pl.multiple_of(tp * 512 + core * 256, 256), 256), :]

    wo_copies = []
    for n, tp in enumerate((topp, tn, tb)):
        wo_copies.append(
            remote(
                wo_h.at[pl.ds(wo_half, 256), pl.ds(pl.multiple_of(tp * 512, 512), 512)],
                wo_rows(t, c), wo_send.at[n], wo_recv.at[t], tp=tp,
            )
        )
    def wo_sends():
        for copy in wo_copies:
            copy.start()

    def square_part(m):
        def part(tp, lo, n):
            return wall.at[tp, m, pl.ds(pl.multiple_of(lo * 4, 256), n * 4), :]

        return part

    def out_part(tp, lo, n):
        return wdo.at[pl.ds(pl.multiple_of(tp * 256 + lo, 64), n), :]

    parts = (square_part(0), square_part(1), square_part(2), out_part)
    PARTS = len(parts)
    mine = c * 128
    theirs = oc * 128

    def wd_direct(p, way):
        if p < 3:
            src = (wdq_h, wdk_h, wdv_h)[p].at[pl.ds(pl.multiple_of(mine * 4, 512), 512), :]
        else:
            src = wdo_h.at[pl.ds(pl.multiple_of(mine, 128), 128), :]
        return remote(src, parts[p](t, mine, 128), wd_send.at[p, way], wd_recv.at[p, way], tp=(tn, tb)[way])

    def wd_start(p):
        for way in range(2):
            wd_direct(p, way).start()

    def wd_first():
        wd_start(0)
        wd_start(1)

    def wd_relay(p, way):
        tp = (tb, tn)[way]
        ref = parts[p](tp, mine + way * 64, 64)
        return remote(ref, ref, wd_send.at[p, 2 + way], wd_recv.at[p, 2 + way], tp=(tn, tb)[way])

    def wd_hand(p, way, core_lo):
        tp = (tb, tn)[way]
        ref = parts[p](tp, core_lo, 128)
        return remote(ref, ref, wd_send.at[p, 4 + way], wd_recv.at[p, 4 + way], seq=sib)

    def wd_hand_relayed(p, way, core_lo):
        ref = parts[p](topp, core_lo + way * 64, 64)
        return remote(ref, ref, wd_send.at[p, 6 + way], wd_recv.at[p, 6 + way], seq=sib)

    def wd_direct_arrived(p, way):
        ref = parts[p]((tb, tn)[way], mine, 128)
        return remote(ref, ref, wd_send.at[p, way], wd_recv.at[p, way], tp=(tn, tb)[way])

    def wd_relay_arrived(p, way):
        ref = parts[p](topp, mine + way * 64, 64)
        return remote(ref, ref, wd_send.at[p, 2 + way], wd_recv.at[p, 2 + way], tp=(tn, tb)[way])

    def wd_pass(p):
        for way in range(2):
            wd_direct_arrived(p, way).wait_recv()
            wd_relay(p, way).start()
            wd_hand(p, way, mine).start()

    def wo_arrived(tp, core, slot):
        ref = wo_rows(tp, core)
        return remote(ref, ref, wo_send.at[0], wo_recv.at[slot], seq=sib)

    wo_sends()
    wd_first()
    loads[3].wait()
    scale = HEAD ** (-0.5) * LOG2E
    for n in range(2):
        both = (dot(normed[...], wqkv[:, 512 + n * 256 : 768 + n * 256]) * scale).astype(BF16)
        q_st[2 * n] = both[:, 0:128]
        q_st[2 * n + 1] = both[:, 128:256]
    for copy in q_copies:
        copy.start()
    q_all[q_slot] = q_st[q_slot]


    for h in range(2):
        m_s[h] = jnp.full((1, PAIR), NEG, F32)
        l_s[h] = jnp.zeros((1, PAIR), F32)
        acc_s[h] = jnp.zeros((HEAD, PAIR), F32)

    def fold(b, masked):
        for h in range(2):
            keys = kv[b, :, 0:128]
            values = kv[b, :, 128:256]
            queries = q_all[2 * h : 2 * h + 2].reshape(PAIR, HEAD)
            scores = dot_nt(keys, queries)
            if masked:
                ahead = (b - (chip // 2 * 2 + h)) * PAIR
                kpos = lax.broadcasted_iota(jnp.int32, (PAIR, PAIR), 0) + ahead
                qpos = lax.broadcasted_iota(jnp.int32, (PAIR, PAIR), 1)
                scores = jnp.where(kpos <= qpos, scores, NEG)
            old = m_s[h]
            top = jnp.maximum(old, jnp.max(scores, axis=0, keepdims=True))
            weights = jnp.exp2(scores - top)
            factor = jnp.exp2(old - top)
            l_s[h] = l_s[h] * factor + jnp.sum(weights, axis=0, keepdims=True)
            acc_s[h] = acc_s[h] * factor + dot_tn(values, weights.astype(BF16))
            m_s[h] = top

    def fold_arrived(b, used):
        @pl.when(used)
        def _():
            remote(
                kv_half(b, other_rows), kv_half(b, other_rows), sib_send.at[b], sib_recv.at[b], seq=sib
            ).wait_recv()

        masked = b // 2 == chip // 2

        @pl.when(jnp.logical_and(used, masked))
        def _():
            fold(b, True)

        @pl.when(jnp.logical_and(used, jnp.logical_not(masked)))
        def _():
            fold(b, False)

    for head in range(4):
        @pl.when(head != q_slot)
        def _():
            remote(q_all.at[head], q_all.at[head], d2d_send.at[0], q_recv.at[head], seq=sib).wait_recv()

    def step(e, before):
        b, valid, used, ways = event(e)

        @pl.when(valid)
        def _():
            kv_copy(b, UP).wait_recv()
            forward(b, ways)

        @pl.when(used)
        def _():
            sib_copy(b).start()

        fold_arrived(before[0], before[1] > 0)

        @pl.when(e == 5)
        def _():
            wd_pass(0)
            wd_start(2)

        @pl.when(e == 9)
        def _():
            wd_pass(1)
            wd_start(3)

        @pl.when(e == 12)
        def _():
            for n, tp in enumerate((topp, tn, tb)):
                remote(wo_rows(tp, c), wo_rows(tp, c), wo_send.at[n], wo_recv.at[tp], seq=sib).wait_recv()
                remote(wo_rows(tp, c), wo_rows(tp, c), wo_send.at[3 + n], wo_recv.at[4 + tp], seq=sib).start()

        return b, used.astype(jnp.int32)

    last = lax.fori_loop(1, 16, step, (first_block, jnp.int32(1)))
    fold_arrived(last[0], last[1] > 0)

    my_lanes = pl.ds(pl.multiple_of(q_slot * HEAD, HEAD), HEAD)

    def att_at(tp, head):
        return att_all.at[tp, :, pl.ds(pl.multiple_of(head * HEAD, HEAD), HEAD)]

    def att_copy(n, group, seq, tp):
        return remote(
            att_st.at[group], att_at(t, q_slot), att_send.at[n], att_recv.at[t, q_slot], seq=seq, tp=tp
        )

    att_copies = [
        att_copy(0, op * 2 + c, mate, t), att_copy(1, op * 2 + oc, mate_sib, t),
        att_copy(2, p * 2 + c, s, tn), att_copy(3, p * 2 + c, s, tb),
        att_copy(4, p * 2 + oc, sib, tn), att_copy(5, p * 2 + oc, sib, tb), att_copy(6, p * 2 + oc, sib, t),
    ]
    for h in range(2):
        heads = acc_s[h] / l_s[h]
        heads = heads * lax.rsqrt(jnp.mean(heads * heads, axis=0, keepdims=True) + 1e-06)
        heads = heads.T.astype(BF16)
        att_st[2 * h] = heads[0:256]
        att_st[2 * h + 1] = heads[256:512]
    for copy in att_copies:
        copy.start()
    att_all[t, :, my_lanes] = att_st[q_slot]

    def att_pass(n, tp, head, to):
        return remote(att_at(tp, head), att_at(tp, head), att_send.at[n], att_recv.at[tp, head], tp=to)

    def att_arrived(tp, head):
        att_pass(0, tp, head, tn).wait_recv()

    mate_copies = []
    for core in range(2):
        for way, to in enumerate((tn, tb)):
            mate_copies.append(att_pass(7 + 2 * core + way, t, op * 2 + core, to))
    for core in range(2):
        att_arrived(t, op * 2 + core)
        mate_copies[2 * core].start()
        mate_copies[2 * core + 1].start()

    loads[10].wait()
    row_level = lax.broadcasted_iota(jnp.int32, (DROWS, LEVELS), 0) % LEVELS
    lane = lax.broadcasted_iota(jnp.int32, (DROWS, LEVELS), 1)
    my_codes = codes_ref[pl.ds(pl.multiple_of(t * QROWS, QROWS), QROWS), :]
    spread = jnp.broadcast_to(my_codes[:, None, :], (QROWS, LEVELS, LEVELS)).reshape(DROWS, LEVELS)
    code = jnp.sum(jnp.where(lane == row_level - 1, spread, 0), axis=-1, keepdims=True)
    level0 = lax.broadcasted_iota(jnp.int32, (DROWS, 1), 0) % LEVELS == 0
    code = jnp.where(level0, -1, code)
    slab_row = lax.broadcasted_iota(jnp.int32, (DROWS, LEVELS), 0) // LEVELS + t * QROWS
    geo = jnp.sum(jnp.where(lane == slab_row, jnp.broadcast_to(geo_ref[...], (DROWS, LEVELS)), 0), axis=-1, keepdims=True)
    code_hot = (lax.broadcasted_iota(jnp.int32, (DROWS, DD), 1) == code).astype(F32).astype(BF16)
    geo_hot = (lax.broadcasted_iota(jnp.int32, (DROWS, 64), 1) == geo).astype(F32).astype(BF16)
    for n in range(4):
        part = slice(n * 256, (n + 1) * 256)
        level = jnp.broadcast_to(level_ref[:, part].astype(F32)[None], (QROWS, LEVELS, 256)).reshape(DROWS, 256)
        hid[:, part] = dot(code_hot, codet[:, part]) + dot(geo_hot, geot_ref[:, part]) + level

    loads[8].wait()
    for n, tp in enumerate((topp, tn, tb)):
        wo_arrived(tp, oc, 4 + tp).wait_recv()

    def project(tp):
        rows = pl.ds(pl.multiple_of(tp * 512, 512), 512)
        return dot(att_all[tp], wo[rows, :])

    att_arrived(t, p * 2 + oc)
    total = frames[:, pl.ds(pl.multiple_of(t * 512, 512), 512)].astype(F32) + project(t)
    relays = []
    for core, head_of in ((0, p * 2), (1, op * 2)):
        for tp, to, odd in ((tb, tn, 0), (tn, tb, 1)):
            relays.append(att_pass(11 + len(relays), tp, head_of + odd, to))
            att_arrived(tp, head_of + odd)
            relays[-1].start()
    for tp, odd in ((tb, 1), (tn, 0)):
        att_arrived(tp, odd)
        att_arrived(tp, 2 + odd)
        total += project(tp)
    for head in range(4):
        att_arrived(topp, head)
    total += project(topp)
    temporal[...] = total.astype(BF16)
    write = pltpu.make_async_copy(temporal, temporal_h, load_sem.at[11])
    write.start()

    wd_pass(2)

    loads[9].wait()
    pick_hot = (lax.broadcasted_iota(jnp.int32, (ROWS, SEQ), 0) == pick_ref[...]).astype(F32).astype(BF16)
    picked = dot_tn(pick_hot, temporal[...]).astype(BF16)
    for n in range(8):
        ctx_st[:, n, :] = dot(picked, wc[:, n * 128 : (n + 1) * 128])
    def ctx_rows(u):
        return ctx_st.at[pl.ds(pl.multiple_of(u * QROWS, QROWS), QROWS)]

    def ctx_copy(n, tp):
        return remote(ctx_rows(tp), ctx_in.at[t], ctx_send.at[n], ctx_recv.at[t], tp=tp)

    ctx_copies = [ctx_copy(n, tp) for n, tp in enumerate((topp, tn, tb))]
    for copy in ctx_copies:
        copy.start()

    wd_pass(3)

    ctx_total = ctx_st[pl.ds(pl.multiple_of(t * QROWS, QROWS), QROWS)].astype(BF16).astype(F32)
    for tp in (tn, tb, topp):
        remote(ctx_in.at[tp], ctx_in.at[tp], ctx_send.at[0], ctx_recv.at[tp], tp=tp).wait_recv()
        ctx_total = ctx_total + ctx_in[tp].astype(BF16).astype(F32)
    ctx_mine[...] = ctx_total.astype(BF16).astype(F32)

    to_tp = s // 8
    stays = to_tp == t
    place = s % 8

    def row_copy(n):
        return remote(ctx_mine.at[n], ctx_rv.at[place], row_send.at[n], row_recv.at[place], seq=t * 8 + n, tp=to_tp)

    def is_self(n):
        return jnp.logical_and(t * 8 + n == s, stays)

    for n in range(QROWS):
        @pl.when(jnp.logical_not(is_self(n)))
        def _():
            row_copy(n).start()

    own_row = pltpu.make_async_copy(ctx_mine.at[place], ctx_rv.at[place], self_sem)

    @pl.when(stays)
    def _():
        own_row.start()
        own_row.wait()

    for n in range(QROWS):
        @pl.when(jnp.logical_not(is_self(n)))
        def _():
            ref = ctx_rv.at[n]
            remote(ref, ref, row_send.at[n], row_recv.at[n], seq=sib).wait_recv()

    for load in loads[4:8]:
        load.wait()

    square = jnp.zeros((DROWS, 1), F32)
    for n in range(8):
        part = slice(n * 128, (n + 1) * 128)
        rows = []
        for r in range(QROWS):
            rows.append(jnp.broadcast_to(ctx_rv[r, n : n + 1, :], (LEVELS, 128)))
        value = hid[:, part] + jnp.concatenate(rows, axis=0)
        hid[:, part] = value
        square += jnp.sum(value * value, axis=-1, keepdims=True)
    factor = lax.rsqrt(square * (1.0 / DD) + 1e-05)
    dn[...] = (hid[...] * factor).astype(BF16)

    dscale = DHEAD ** (-0.5) * LOG2E
    lrow = lax.broadcasted_iota(jnp.int32, (128, 128), 0)
    lcol = lax.broadcasted_iota(jnp.int32, (128, 128), 1)
    allowed = jnp.logical_and(lrow // LEVELS == lcol // LEVELS, lrow <= lcol)

    for n, g in enumerate((t, tb, tn, topp)):
        if n == 1 or n == 2:
            for p in range(3):
                wd_hand(p, n - 1, theirs).wait_recv()
        if n == 2:
            for p in range(PARTS):
                for way in range(2):
                    wd_relay_arrived(p, way).wait_recv()
                    wd_hand_relayed(p, way, mine).start()
        if n == 3:
            for p in range(3):
                for way in range(2):
                    wd_hand_relayed(p, way, theirs).wait_recv()
        queries = (dot(dn[...], wall[g, 0]) * dscale).astype(BF16)
        keys = dot(dn[...], wall[g, 1]).astype(BF16)
        values = dot(dn[...], wall[g, 2]).astype(BF16)
        for r in range(2):
            rows = slice(r * 128, (r + 1) * 128)
            outs = []
            for h in range(4):
                part = slice(h * DHEAD, (h + 1) * DHEAD)
                scores = dot_nt(keys[rows, part], queries[rows, part])
                scores = jnp.where(allowed, scores, NEG)
                top = jnp.max(scores, axis=0, keepdims=True)
                weights = jnp.exp2(scores - top)
                sums = jnp.sum(weights, axis=0, keepdims=True)
                heads = dot_tn(values[rows, part], weights.astype(BF16)) / sums
                heads = heads * lax.rsqrt(jnp.mean(heads * heads, axis=0, keepdims=True) + 1e-06)
                outs.append(heads)
            datt[rows, pl.ds(pl.multiple_of(g * 256, 256), 256)] = jnp.concatenate(outs, axis=0).T.astype(BF16)

    for way in range(2):
        wd_hand(3, way, theirs).wait_recv()
        wd_hand_relayed(3, way, theirs).wait_recv()

    def out_tile(tp):
        part = pl.ds(pl.multiple_of(tp * 256, 256), 256)
        return (dot(datt[...], wdo[:, part]) + hid[:, part]).astype(BF16)

    def out_rows(tp):
        return depth_h.at[pl.ds(pl.multiple_of(tp * DROWS, DROWS), DROWS), :]

    out_copies = []
    for n, tp in enumerate((topp, tn, tb)):
        osend[n] = out_tile(tp)
        copy = remote(osend.at[n], out_rows(t), out_send.at[n], out_recv.at[t], tp=tp)
        copy.start()
        out_copies.append(copy)
    osend[3] = out_tile(t)
    own_out = pltpu.make_async_copy(osend.at[3], out_rows(t), load_sem.at[12])
    own_out.start()

    for copy in [kv_mate, kv_sib] + q_copies + wo_copies + att_copies + mate_copies + relays:
        copy.wait_send()
    for n, tp in enumerate((topp, tn, tb)):
        remote(wo_rows(tp, c), wo_rows(tp, c), wo_send.at[3 + n], wo_recv.at[4 + tp], seq=sib).wait_send()
    for p in range(PARTS):
        for way in range(2):
            wd_direct(p, way).wait_send()
            wd_relay(p, way).wait_send()
            wd_hand(p, way, mine).wait_send()
            wd_hand_relayed(p, way, mine).wait_send()

    def sent(e, carry):
        b, _, used, ways = event(e)

        @pl.when(jnp.logical_and(used, e > 0))
        def _():
            sib_copy(b).wait_send()

        for way in range(3):
            @pl.when(ways[way])
            def _():
                kv_copy(b, way).wait_send()

        return carry

    lax.fori_loop(0, 16, sent, 0)

    for copy in ctx_copies:
        copy.wait_send()
    for n in range(QROWS):
        @pl.when(jnp.logical_not(is_self(n)))
        def _():
            row_copy(n).wait_send()

    write.wait()
    own_out.wait()
    for n, tp in enumerate((topp, tn, tb)):
        out_copies[n].wait_send()
    for tp in (topp, tn, tb):
        remote(osend.at[0], out_rows(tp), out_send.at[0], out_recv.at[tp], tp=tp).wait_recv()


def hand_on(temporal_in, depth_in, temporal_out, depth_out):
    temporal_out[...] = temporal_in[...]
    depth_out[...] = depth_in[...]


def body(
    frames, w_query, w_key, w_value, w_out, frame_pick, codes, geo_ids, geo_table, w_context, code_table,
    level_table, wd_query, wd_key, wd_value, wd_out,
):
    hbm = pl.BlockSpec(memory_space=pl.ANY)
    vmem = pl.BlockSpec(memory_space=pltpu.VMEM)
    sem = pltpu.SemaphoreType.DMA
    temporal, depth = pl.pallas_call(
        kernel,
        out_shape=(
            jax.ShapeDtypeStruct((ROWS, 512), BF16),
            jax.ShapeDtypeStruct((SEQ * LEVELS, 256), BF16),
        ),
        in_specs=[hbm, hbm, hbm, hbm, hbm, vmem, vmem, vmem, vmem, hbm, hbm, vmem, hbm, hbm, hbm, hbm],
        out_specs=(hbm, hbm),
        scratch_shapes=[
            pltpu.VMEM((ROWS, D), BF16),
            pltpu.VMEM((ROWS, D), BF16),
            pltpu.VMEM((D, 1024), BF16),
            pltpu.VMEM((2, ROWS, 256), BF16),
            pltpu.VMEM((4, ROWS, HEAD), BF16),
            pltpu.VMEM((4, ROWS, HEAD), BF16),
            pltpu.VMEM((CHIPS, PAIR, 256), BF16),
            pltpu.VMEM((2, 1, PAIR), F32),
            pltpu.VMEM((2, 1, PAIR), F32),
            pltpu.VMEM((2, HEAD, PAIR), F32),
            pltpu.VMEM((4, ROWS, HEAD), BF16),
            pltpu.VMEM((TP, ROWS, 512), BF16),
            pltpu.VMEM((D, 512), BF16),
            pltpu.VMEM((ROWS, 512), BF16),
            pltpu.VMEM((512, DD), BF16),
            pltpu.VMEM((SEQ, 8, 128), F32),
            pltpu.VMEM((TP, QROWS, 8, 128), F32),
            pltpu.VMEM((QROWS, 8, 128), F32),
            pltpu.VMEM((QROWS, 8, 128), F32),
            pltpu.VMEM((DD, DD), BF16),
            pltpu.VMEM((TP, 3, DD, 256), BF16),
            pltpu.VMEM((DD, DD), BF16),
            pltpu.VMEM((DROWS, DD), F32),
            pltpu.VMEM((DROWS, DD), BF16),
            pltpu.VMEM((DROWS, DD), BF16),
            pltpu.VMEM((TP, DROWS, 256), BF16),
            sem((13,)),
            sem((5,)),
            sem((4,)),
            sem((3, CHIPS)),
            sem((CHIPS,)),
            sem((CHIPS,)),
            sem((CHIPS,)),
            sem((6,)),
            sem((8,)),
            sem((4, 8)),
            sem((4, 8)),
            sem((15,)),
            sem((TP, 4)),
            sem((3,)),
            sem((TP,)),
            sem((QROWS,)),
            sem((QROWS,)),
            sem((3,)),
            sem((TP,)),
            sem(()),
        ],
        compiler_params=pltpu.CompilerParams(
            collective_id=0, has_side_effects=True, vmem_limit_bytes=58 * 1024 * 1024
        ),
        name="codec_layers",
    )(
        frames, w_query, w_key, w_value, w_out, frame_pick.reshape(1, SEQ), codes, geo_ids.reshape(1, SEQ),
        geo_table, w_context, code_table, level_table, wd_query, wd_key, wd_value, wd_out,
    )
    temporal, depth = pl.pallas_call(
        hand_on,
        out_shape=(
            jax.ShapeDtypeStruct((ROWS, 512), BF16),
            jax.ShapeDtypeStruct((SEQ * LEVELS, 256), BF16),
        ),
        in_specs=[vmem, vmem],
        out_specs=(vmem, vmem),
        compiler_params=pltpu.CompilerParams(vmem_limit_bytes=58 * 1024 * 1024),
        name="hand_on",
    )(temporal, depth)
    return temporal, depth.reshape(SEQ, LEVELS, 256)


def solution(mesh):
    return jax.shard_map(
        body,
        mesh=mesh,
        in_specs=(
            P(("dp", "seq"), None),
            P(None, "tp"),
            P(None, "tp"),
            P(None, "tp"),
            P("tp", None),
            P(("dp", "seq"), None, None),
            P(("dp", "seq"), None),
            P(("dp", "seq")),
            P(),
            P("tp", None),
            P(),
            P(),
            P(None, "tp"),
            P(None, "tp"),
            P(None, "tp"),
            P("tp", None),
        ),
        out_specs=(P(("dp", "seq"), "tp"), P(("dp", "seq"), None, "tp")),
        check_vma=False,
    )
```

time: 106 us -> 97.4 us (0.919)
  local copies, waits for them, and re-layouts: 4.88 us -> 0 us
  Pallas kernels: 99.8 us -> 96.4 us
    pallas_call x1, Pallas kernels: 99.8 us -> 94.4 us  [body(): pl.pallas_call(kernel, out_shape=(jax.ShapeDtypeStruct((ROWS, 512), BF16)...]
    unnamed x2 -> x0, local copies, waits for them, and re-layouts: 3.54 us -> none
    pallas_call x0 -> x1, Pallas kernels: none -> 2.02 us  [body(): pl.pallas_call(hand_on, out_shape=(jax.ShapeDtypeStruct((ROWS, 512), BF16...]
    reshape x1 -> x0, local copies, waits for them, and re-layouts: 1.34 us -> none  [body(): frame_pick.reshape(SEQ, 1)]
where the time goes in v2:
time: 97.4 us; the launch traced here: 97.1 us
  Pallas kernels  96.4 us (99%)
    pallas_call x1, Pallas kernels, body(): pl.pallas_call(kernel, out_shape=(jax.ShapeDtypeStruct((ROWS, 512), BF16)...  94.4 us
    pallas_call x1, Pallas kernels, body(): pl.pallas_call(hand_on, out_shape=(jax.ShapeDtypeStruct((ROWS, 512), BF16...  2.02 us

profile of v2, /device:TPU:1, one launch (start us, length us, event | category | flops | bytes accessed | tf_op | source)
XLA Modules:
  0.0 97.1 jit_solution(13645885437714261744)
XLA Ops:
  0.6 94.4 %codec_layers.1 = (bf16[256,512]{1,0:T(8,128)(2,1)}, bf16[1024,256]{1,0:T(8,128)(2,1)}) custom-call(bf16[256,2048]{1,0:T(8,128)(2,1)} %frames_h.1, bf16[2048,512]{1,0:T(8,128)(2,1)} %wq_h.1, bf16[2048,256]{1,0:T(8,128)(2,1)} %wk_h.1, bf16[2048,256]{1,0:T(8,128)(2,1)} %wv_h.1, bf16[512,2048]{1,0:T(8,128)(2,1)} %wo_h.1, s32[1,32]{1,0:T(1,128)} %bitcast.3, ...), custom_call_target="tpu_custom_call" | custom-call | tf_op jit(solution)/shard_map/codec_layers/pallas_call | solution.py:660
  95.0 2.0 %hand_on.1 = (bf16[256,512]{1,0:T(8,128)(2,1)}, bf16[1024,256]{1,0:T(8,128)(2,1)}) custom-call(bf16[256,512]{1,0:T(8,128)(2,1)} %get-tuple-element.6.temporal_in, bf16[1024,256]{1,0:T(8,128)(2,1)} %get-tuple-element.7.depth_in), custom_call_target="tpu_custom_call" | custom-call | tf_op jit(solution)/shard_map/hand_on/pallas_call | solution.py:724

commit v3 on v2

--- a/solution.py
+++ b/solution.py
@@ -27,23 +27,26 @@
 DROWS = QROWS * LEVELS
 NEG = -1e30
 
-EVENTS = (
-    ((0, 0), (0, 1), (1, 0), (1, 1), (0, 2), (0, 3)),
-    ((1, 0), (1, 1), (0, 0), (0, 1), (1, 2), (0, 2), (1, 3), (0, 3)),
-    ((2, 0), (2, 1), (1, 0), (0, 0), (1, 1), (0, 1), (2, 2), (1, 2), (0, 2), (2, 3), (1, 3), (0, 3)),
+GROUPS = (
+    (((0, 0),), ((0, 1), (1, 0)), ((1, 1), (0, 2)), (), ((0, 3),), (), ()),
+    (((1, 0),), ((1, 1), (0, 0)), ((0, 1), (1, 2)), ((0, 2),), ((1, 3),), ((0, 3),), ()),
     (
-        (3, 0), (3, 1), (2, 0), (0, 0), (2, 1), (0, 1), (1, 0), (3, 2),
-        (2, 2), (1, 1), (1, 2), (0, 2), (3, 3), (2, 3), (0, 3), (1, 3),
+        ((2, 0),), ((2, 1), (1, 0)), ((1, 1), (0, 0), (2, 2)), ((1, 2), (0, 1)), ((0, 2), (2, 3)), ((1, 3),),
+        ((0, 3),),
+    ),
+    (
+        ((3, 0),), ((3, 1), (2, 0), (0, 0)), ((2, 1), (0, 1), (3, 2)), ((2, 2), (1, 0)), ((1, 2), (1, 1), (3, 3)),
+        ((2, 3), (0, 2)), ((1, 3), (0, 3)),
     ),
 )
 ORDER = tuple(tuple(z ^ k for k in range(4)) for z in range(4))
 ACROSS, UP, DOWN = range(3)
 
 
-def event_fields(y, z, e):
-    if e >= len(EVENTS[y]):
+def event_fields(y, z, group, n):
+    if n >= len(GROUPS[y][group]):
         return 0
-    br, k = EVENTS[y][e]
+    br, k = GROUPS[y][group][n]
     bz = ORDER[z][k]
     if br == 3 and bz // 2 > z // 2:
         return 0
@@ -59,10 +62,8 @@
 
 
 EVENT_WORDS = tuple(
-    tuple(
-        sum(event_fields(n // 4, n % 4, 3 * w + i) << (10 * i) for i in range(3)) for n in range(CHIPS)
-    )
-    for w in range(6)
+    tuple(sum(event_fields(n // 4, n % 4, w, i) << (10 * i) for i in range(3)) for n in range(CHIPS))
+    for w in range(7)
 )
 
 
@@ -89,9 +90,9 @@
     frames_h, wq_h, wk_h, wv_h, wo_h, pick_ref, codes_ref, geo_ref, geot_ref, wc_h, codet_h, level_ref,
     wdq_h, wdk_h, wdv_h, wdo_h,
     temporal_h, depth_h,
-    frames, normed, wqkv, kv_st, q_st, q_all, kv, m_s, l_s, acc_s, att_st, att_all, wo, temporal, wc, ctx_st, ctx_in, ctx_mine, ctx_rv,
+    frames, normed, wqkv, kv_st, q_st, q_all, kv, m_s, l_s, acc_s, att_st, att, far_st, far_in, near_st, near_in, wo, temporal, wc, ctx_st, ctx_in, ctx_mine, ctx_rv,
     codet, wall, wdo, hid, dn, datt, osend,
-    load_sem, d2d_send, q_recv, kv_send, kv_recv, sib_send, sib_recv, wo_send, wo_recv, wd_send, wd_recv, att_send, att_recv,
+    load_sem, d2d_send, q_recv, kv_send, kv_recv, sib_send, sib_recv, wd_send, wd_recv, att_send, att_recv, sum_send, sum_recv,
     ctx_send, ctx_recv, row_send, row_recv, out_send, out_recv, self_sem,
 ):
     s = lax.axis_index("seq")
@@ -113,9 +114,6 @@
             device_id_type=MESH,
         )
 
-    def cols(ref, start, size):
-        return ref.at[:, pl.ds(pl.multiple_of(start * size, size), size)]
-
     loads = [
         pltpu.make_async_copy(frames_h, frames, load_sem.at[0]),
         pltpu.make_async_copy(wk_h, wqkv.at[:, 0:256], load_sem.at[1]),
@@ -125,9 +123,7 @@
         pltpu.make_async_copy(wdk_h, wall.at[t, 1], load_sem.at[5]),
         pltpu.make_async_copy(wdv_h, wall.at[t, 2], load_sem.at[6]),
         pltpu.make_async_copy(wdo_h, wdo.at[pl.ds(pl.multiple_of(t * 256, 256), 256), :], load_sem.at[7]),
-        pltpu.make_async_copy(
-            cols(wo_h, t, 512), wo.at[pl.ds(pl.multiple_of(t * 512, 512), 512), :], load_sem.at[8]
-        ),
+        pltpu.make_async_copy(wo_h, wo, load_sem.at[8]),
         pltpu.make_async_copy(wc_h, wc, load_sem.at[9]),
         pltpu.make_async_copy(codet_h, codet, load_sem.at[10]),
     ]
@@ -203,14 +199,12 @@
 
     words = [pick(chip, table) for table in EVENT_WORDS]
 
-    def event(e):
-        word = pick(e // 3, words)
-        place = e % 3
-        bits = jnp.where(place == 0, word, jnp.where(place == 1, word // 1024, word // (1024 * 1024)))
-        flags = [(bits // (16 << n)) % 2 == 1 for n in range(5)]
+    def event(word, n):
+        bits = word // (1024**n)
+        flags = [(bits // (16 << i)) % 2 == 1 for i in range(5)]
         return bits % 16, flags[0], flags[1], flags[2:]
 
-    first_block, _, _, first_ways = event(jnp.int32(0))
+    first_block, _, _, first_ways = event(words[0], 0)
     forward(first_block, first_ways)
 
     q_slot = p * 2 + c
@@ -221,23 +215,6 @@
     q_copies = [
         q_copy(0, mate, op * 2 + c), q_copy(1, mate_sib, op * 2 + oc), q_copy(2, sib, p * 2 + oc),
     ]
-
-    wo_half = pl.multiple_of(c * 256, 256)
-
-    def wo_rows(tp, core):
-        return wo.at[pl.ds(pl.multiple_of(tp * 512 + core * 256, 256), 256), :]
-
-    wo_copies = []
-    for n, tp in enumerate((topp, tn, tb)):
-        wo_copies.append(
-            remote(
-                wo_h.at[pl.ds(wo_half, 256), pl.ds(pl.multiple_of(tp * 512, 512), 512)],
-                wo_rows(t, c), wo_send.at[n], wo_recv.at[t], tp=tp,
-            )
-        )
-    def wo_sends():
-        for copy in wo_copies:
-            copy.start()
 
     def square_part(m):
         def part(tp, lo, n):
@@ -290,17 +267,17 @@
         ref = parts[p](topp, mine + way * 64, 64)
         return remote(ref, ref, wd_send.at[p, 2 + way], wd_recv.at[p, 2 + way], tp=(tn, tb)[way])
 
+    def wd_pass_relayed(p):
+        for way in range(2):
+            wd_relay_arrived(p, way).wait_recv()
+            wd_hand_relayed(p, way, mine).start()
+
     def wd_pass(p):
         for way in range(2):
             wd_direct_arrived(p, way).wait_recv()
             wd_relay(p, way).start()
             wd_hand(p, way, mine).start()
 
-    def wo_arrived(tp, core, slot):
-        ref = wo_rows(tp, core)
-        return remote(ref, ref, wo_send.at[0], wo_recv.at[slot], seq=sib)
-
-    wo_sends()
     wd_first()
     loads[3].wait()
     scale = HEAD ** (-0.5) * LOG2E
@@ -359,55 +336,48 @@
         def _():
             remote(q_all.at[head], q_all.at[head], d2d_send.at[0], q_recv.at[head], seq=sib).wait_recv()
 
-    def step(e, before):
-        b, valid, used, ways = event(e)
-
-        @pl.when(valid)
-        def _():
-            kv_copy(b, UP).wait_recv()
-            forward(b, ways)
-
-        @pl.when(used)
-        def _():
-            sib_copy(b).start()
-
-        fold_arrived(before[0], before[1] > 0)
-
-        @pl.when(e == 5)
+    def step(w, carry):
+        word = pick(w, words)
+        for n in range(3):
+            b, valid, used, ways = event(word, n)
+
+            @pl.when(jnp.logical_and(valid, w > 0))
+            def _():
+                kv_copy(b, UP).wait_recv()
+                forward(b, ways)
+
+            @pl.when(jnp.logical_and(used, w > 0))
+            def _():
+                sib_copy(b).start()
+
+        def fold_one(n, carry):
+            bits = jnp.where(n == 0, word, jnp.where(n == 1, word // 1024, word // (1024 * 1024)))
+            fold_arrived(bits % 16, (bits // 32) % 2 == 1)
+            return carry
+
+        lax.fori_loop(0, 3, fold_one, 0)
+
+        @pl.when(w == 2)
         def _():
             wd_pass(0)
             wd_start(2)
 
-        @pl.when(e == 9)
+        @pl.when(w == 4)
         def _():
             wd_pass(1)
             wd_start(3)
 
-        @pl.when(e == 12)
-        def _():
-            for n, tp in enumerate((topp, tn, tb)):
-                remote(wo_rows(tp, c), wo_rows(tp, c), wo_send.at[n], wo_recv.at[tp], seq=sib).wait_recv()
-                remote(wo_rows(tp, c), wo_rows(tp, c), wo_send.at[3 + n], wo_recv.at[4 + tp], seq=sib).start()
-
-        return b, used.astype(jnp.int32)
-
-    last = lax.fori_loop(1, 16, step, (first_block, jnp.int32(1)))
-    fold_arrived(last[0], last[1] > 0)
+        return carry
+
+    lax.fori_loop(0, 7, step, 0)
 
     my_lanes = pl.ds(pl.multiple_of(q_slot * HEAD, HEAD), HEAD)
 
-    def att_at(tp, head):
-        return att_all.at[tp, :, pl.ds(pl.multiple_of(head * HEAD, HEAD), HEAD)]
-
-    def att_copy(n, group, seq, tp):
-        return remote(
-            att_st.at[group], att_at(t, q_slot), att_send.at[n], att_recv.at[t, q_slot], seq=seq, tp=tp
-        )
+    def att_copy(n, group, seq):
+        return remote(att_st.at[group], att.at[:, my_lanes], att_send.at[n], att_recv.at[q_slot], seq=seq)
 
     att_copies = [
-        att_copy(0, op * 2 + c, mate, t), att_copy(1, op * 2 + oc, mate_sib, t),
-        att_copy(2, p * 2 + c, s, tn), att_copy(3, p * 2 + c, s, tb),
-        att_copy(4, p * 2 + oc, sib, tn), att_copy(5, p * 2 + oc, sib, tb), att_copy(6, p * 2 + oc, sib, t),
+        att_copy(0, op * 2 + c, mate), att_copy(1, op * 2 + oc, mate_sib), att_copy(2, p * 2 + oc, sib),
     ]
     for h in range(2):
         heads = acc_s[h] / l_s[h]
@@ -417,22 +387,7 @@
         att_st[2 * h + 1] = heads[256:512]
     for copy in att_copies:
         copy.start()
-    att_all[t, :, my_lanes] = att_st[q_slot]
-
-    def att_pass(n, tp, head, to):
-        return remote(att_at(tp, head), att_at(tp, head), att_send.at[n], att_recv.at[tp, head], tp=to)
-
-    def att_arrived(tp, head):
-        att_pass(0, tp, head, tn).wait_recv()
-
-    mate_copies = []
-    for core in range(2):
-        for way, to in enumerate((tn, tb)):
-            mate_copies.append(att_pass(7 + 2 * core + way, t, op * 2 + core, to))
-    for core in range(2):
-        att_arrived(t, op * 2 + core)
-        mate_copies[2 * core].start()
-        mate_copies[2 * core + 1].start()
+    att[:, my_lanes] = att_st[q_slot]
 
     loads[10].wait()
     row_level = lax.broadcasted_iota(jnp.int32, (DROWS, LEVELS), 0) % LEVELS
@@ -452,28 +407,43 @@
         hid[:, part] = dot(code_hot, codet[:, part]) + dot(geo_hot, geot_ref[:, part]) + level
 
     loads[8].wait()
-    for n, tp in enumerate((topp, tn, tb)):
-        wo_arrived(tp, oc, 4 + tp).wait_recv()
+    for head in range(4):
+        @pl.when(head != q_slot)
+        def _():
+            ref = att.at[:, head * HEAD : (head + 1) * HEAD]
+            remote(ref, ref, att_send.at[0], att_recv.at[head], seq=sib).wait_recv()
 
     def project(tp):
-        rows = pl.ds(pl.multiple_of(tp * 512, 512), 512)
-        return dot(att_all[tp], wo[rows, :])
-
-    att_arrived(t, p * 2 + oc)
+        return dot(att[...], wo[:, pl.ds(pl.multiple_of(tp * 512, 512), 512)])
+
+    def far_copy(way):
+        return remote(far_st.at[way], far_in.at[way], sum_send.at[way], sum_recv.at[way], tp=(tn, tb)[way])
+
+    def near_copy(way, part):
+        n = 2 + 2 * way + part
+        return remote(
+            near_st.at[way, part], near_in.at[way, part], sum_send.at[n], sum_recv.at[n], tp=(tn, tb)[way]
+        )
+
+    far = project(topp).astype(BF16)
+    for way in range(2):
+        far_st[way] = far[way * 128 : way * 128 + 128]
+        far_copy(way).start()
+    near = [project(tn), project(tb)]
+    near_st[0, 1] = near[0][128:256].astype(BF16)
+    near_copy(0, 1).start()
+    near_st[1, 0] = near[1][0:128].astype(BF16)
+    near_copy(1, 0).start()
     total = frames[:, pl.ds(pl.multiple_of(t * 512, 512), 512)].astype(F32) + project(t)
-    relays = []
-    for core, head_of in ((0, p * 2), (1, op * 2)):
-        for tp, to, odd in ((tb, tn, 0), (tn, tb, 1)):
-            relays.append(att_pass(11 + len(relays), tp, head_of + odd, to))
-            att_arrived(tp, head_of + odd)
-            relays[-1].start()
-    for tp, odd in ((tb, 1), (tn, 0)):
-        att_arrived(tp, odd)
-        att_arrived(tp, 2 + odd)
-        total += project(tp)
-    for head in range(4):
-        att_arrived(topp, head)
-    total += project(topp)
+    for way in range(2):
+        far_copy(way).wait_recv()
+        passing = near[way][way * 128 : way * 128 + 128] + far_in[way].astype(F32)
+        near_st[way, way] = passing.astype(BF16)
+        near_copy(way, way).start()
+    for way in range(2):
+        for part in range(2):
+            near_copy(way, part).wait_recv()
+    total += near_in[0].reshape(ROWS, 512).astype(F32) + near_in[1].reshape(ROWS, 512).astype(F32)
     temporal[...] = total.astype(BF16)
     write = pltpu.make_async_copy(temporal, temporal_h, load_sem.at[11])
     write.start()
@@ -495,6 +465,8 @@
     for copy in ctx_copies:
         copy.start()
 
+    wd_pass_relayed(0)
+    wd_pass_relayed(1)
     wd_pass(3)
 
     ctx_total = ctx_st[pl.ds(pl.multiple_of(t * QROWS, QROWS), QROWS)].astype(BF16).astype(F32)
@@ -555,11 +527,10 @@
         if n == 1 or n == 2:
             for p in range(3):
                 wd_hand(p, n - 1, theirs).wait_recv()
-        if n == 2:
-            for p in range(PARTS):
-                for way in range(2):
-                    wd_relay_arrived(p, way).wait_recv()
-                    wd_hand_relayed(p, way, mine).start()
+        if n == 1:
+            wd_pass_relayed(2)
+        if n == 3:
+            wd_pass_relayed(3)
         if n == 3:
             for p in range(3):
                 for way in range(2):
@@ -603,10 +574,9 @@
     own_out = pltpu.make_async_copy(osend.at[3], out_rows(t), load_sem.at[12])
     own_out.start()
 
-    for copy in [kv_mate, kv_sib] + q_copies + wo_copies + att_copies + mate_copies + relays:
+    sums = [far_copy(0), far_copy(1)] + [near_copy(way, part) for way in range(2) for part in range(2)]
+    for copy in [kv_mate, kv_sib] + q_copies + att_copies + sums:
         copy.wait_send()
-    for n, tp in enumerate((topp, tn, tb)):
-        remote(wo_rows(tp, c), wo_rows(tp, c), wo_send.at[3 + n], wo_recv.at[4 + tp], seq=sib).wait_send()
     for p in range(PARTS):
         for way in range(2):
             wd_direct(p, way).wait_send()
@@ -614,21 +584,23 @@
             wd_hand(p, way, mine).wait_send()
             wd_hand_relayed(p, way, mine).wait_send()
 
-    def sent(e, carry):
-        b, _, used, ways = event(e)
-
-        @pl.when(jnp.logical_and(used, e > 0))
-        def _():
-            sib_copy(b).wait_send()
-
-        for way in range(3):
-            @pl.when(ways[way])
+    def sent(w, carry):
+        word = pick(w, words)
+        for n in range(3):
+            b, _, used, ways = event(word, n)
+
+            @pl.when(jnp.logical_and(used, w > 0))
             def _():
-                kv_copy(b, way).wait_send()
+                sib_copy(b).wait_send()
+
+            for way in range(3):
+                @pl.when(ways[way])
+                def _():
+                    kv_copy(b, way).wait_send()
 
         return carry
 
-    lax.fori_loop(0, 16, sent, 0)
+    lax.fori_loop(0, 7, sent, 0)
 
     for copy in ctx_copies:
         copy.wait_send()
@@ -677,8 +649,12 @@
             pltpu.VMEM((2, 1, PAIR), F32),
             pltpu.VMEM((2, HEAD, PAIR), F32),
             pltpu.VMEM((4, ROWS, HEAD), BF16),
-            pltpu.VMEM((TP, ROWS, 512), BF16),
-            pltpu.VMEM((D, 512), BF16),
+            pltpu.VMEM((ROWS, 512), BF16),
+            pltpu.VMEM((2, 128, 512), BF16),
+            pltpu.VMEM((2, 128, 512), BF16),
+            pltpu.VMEM((2, 2, 128, 512), BF16),
+            pltpu.VMEM((2, 2, 128, 512), BF16),
+            pltpu.VMEM((512, D), BF16),
             pltpu.VMEM((ROWS, 512), BF16),
             pltpu.VMEM((512, DD), BF16),
             pltpu.VMEM((SEQ, 8, 128), F32),
@@ -699,12 +675,12 @@
             sem((CHIPS,)),
             sem((CHIPS,)),
             sem((CHIPS,)),
-            sem((6,)),
-            sem((8,)),
             sem((4, 8)),
             sem((4, 8)),
-            sem((15,)),
-            sem((TP, 4)),
+            sem((3,)),
+            sem((4,)),
+            sem((6,)),
+            sem((6,)),
             sem((3,)),
             sem((TP,)),
             sem((QROWS,)),

time: 97.4 us -> 97.3 us (level)
  no operation moved by 1% of the time
where the time goes in v3:
time: 97.3 us; the launch traced here: 96.8 us
  Pallas kernels  96.2 us (99%)
    pallas_call x1, Pallas kernels, body(): pl.pallas_call(kernel, out_shape=(jax.ShapeDtypeStruct((ROWS, 512), BF16)...  94.1 us
    pallas_call x1, Pallas kernels, body(): pl.pallas_call(hand_on, out_shape=(jax.ShapeDtypeStruct((ROWS, 512), BF16...  2.02 us

profile of v3, /device:TPU:1, one launch (start us, length us, event | category | flops | bytes accessed | tf_op | source)
XLA Modules:
  0.0 96.8 jit_solution(12913274903741714266)
XLA Ops:
  0.6 94.1 %codec_layers.1 = (bf16[256,512]{1,0:T(8,128)(2,1)}, bf16[1024,256]{1,0:T(8,128)(2,1)}) custom-call(bf16[256,2048]{1,0:T(8,128)(2,1)} %frames_h.1, bf16[2048,512]{1,0:T(8,128)(2,1)} %wq_h.1, bf16[2048,256]{1,0:T(8,128)(2,1)} %wk_h.1, bf16[2048,256]{1,0:T(8,128)(2,1)} %wv_h.1, bf16[512,2048]{1,0:T(8,128)(2,1)} %wo_h.1, s32[1,32]{1,0:T(1,128)} %bitcast.3, ...), custom_call_target="tpu_custom_call" | custom-call | tf_op jit(solution)/shard_map/codec_layers/pallas_call | solution.py:632
  94.8 2.0 %hand_on.1 = (bf16[256,512]{1,0:T(8,128)(2,1)}, bf16[1024,256]{1,0:T(8,128)(2,1)}) custom-call(bf16[256,512]{1,0:T(8,128)(2,1)} %get-tuple-element.6.temporal_in, bf16[1024,256]{1,0:T(8,128)(2,1)} %get-tuple-element.7.depth_in), custom_call_target="tpu_custom_call" | custom-call | tf_op jit(solution)/shard_map/hand_on/pallas_call | solution.py:700

commit v4 on v3

--- a/solution.py
+++ b/solution.py
@@ -440,6 +440,7 @@
         passing = near[way][way * 128 : way * 128 + 128] + far_in[way].astype(F32)
         near_st[way, way] = passing.astype(BF16)
         near_copy(way, way).start()
+    wd_pass(2)
     for way in range(2):
         for part in range(2):
             near_copy(way, part).wait_recv()
@@ -448,8 +449,6 @@
     write = pltpu.make_async_copy(temporal, temporal_h, load_sem.at[11])
     write.start()
 
-    wd_pass(2)
-
     loads[9].wait()
     pick_hot = (lax.broadcasted_iota(jnp.int32, (ROWS, SEQ), 0) == pick_ref[...]).astype(F32).astype(BF16)
     picked = dot_tn(pick_hot, temporal[...]).astype(BF16)
@@ -467,13 +466,13 @@
 
     wd_pass_relayed(0)
     wd_pass_relayed(1)
-    wd_pass(3)
-
     ctx_total = ctx_st[pl.ds(pl.multiple_of(t * QROWS, QROWS), QROWS)].astype(BF16).astype(F32)
     for tp in (tn, tb, topp):
         remote(ctx_in.at[tp], ctx_in.at[tp], ctx_send.at[0], ctx_recv.at[tp], tp=tp).wait_recv()
         ctx_total = ctx_total + ctx_in[tp].astype(BF16).astype(F32)
     ctx_mine[...] = ctx_total.astype(BF16).astype(F32)
+
+    wd_pass(3)
 
     to_tp = s // 8
     stays = to_tp == t

time: 97.3 us -> 95.7 us (0.984)
  Pallas kernels: 96.2 us -> 94.9 us
    pallas_call x1, Pallas kernels: 94.1 us -> 92.9 us  [body(): pl.pallas_call(kernel, out_shape=(jax.ShapeDtypeStruct((ROWS, 512), BF16)...]
where the time goes in v4:
time: 95.7 us; the launch traced here: 95.5 us
  Pallas kernels  94.9 us (99%)
    pallas_call x1, Pallas kernels, body(): pl.pallas_call(kernel, out_shape=(jax.ShapeDtypeStruct((ROWS, 512), BF16)...  92.9 us
    pallas_call x1, Pallas kernels, body(): pl.pallas_call(hand_on, out_shape=(jax.ShapeDtypeStruct((ROWS, 512), BF16...  2.02 us

profile of v4, /device:TPU:1, one launch (start us, length us, event | category | flops | bytes accessed | tf_op | source)
XLA Modules:
  0.0 95.5 jit_solution(6487538972617696319)
XLA Ops:
  0.6 92.9 %codec_layers.1 = (bf16[256,512]{1,0:T(8,128)(2,1)}, bf16[1024,256]{1,0:T(8,128)(2,1)}) custom-call(bf16[256,2048]{1,0:T(8,128)(2,1)} %frames_h.1, bf16[2048,512]{1,0:T(8,128)(2,1)} %wq_h.1, bf16[2048,256]{1,0:T(8,128)(2,1)} %wk_h.1, bf16[2048,256]{1,0:T(8,128)(2,1)} %wv_h.1, bf16[512,2048]{1,0:T(8,128)(2,1)} %wo_h.1, s32[1,32]{1,0:T(1,128)} %bitcast.3, ...), custom_call_target="tpu_custom_call" | custom-call | tf_op jit(solution)/shard_map/codec_layers/pallas_call | solution.py:631
  93.5 2.0 %hand_on.1 = (bf16[256,512]{1,0:T(8,128)(2,1)}, bf16[1024,256]{1,0:T(8,128)(2,1)}) custom-call(bf16[256,512]{1,0:T(8,128)(2,1)} %get-tuple-element.6.temporal_in, bf16[1024,256]{1,0:T(8,128)(2,1)} %get-tuple-element.7.depth_in), custom_call_target="tpu_custom_call" | custom-call | tf_op jit(solution)/shard_map/hand_on/pallas_call | solution.py:699
